TPU v7x, 32 devices: a whole 2x2x4 slice. The times are simulated.
32 devices in a mesh: dp: 2 (over x), fsdp: 16 (over z, y, core).
Axes of the slice: x: 2, y: 2, z: 4, core: 2. Of those that a mesh axis runs over, the one named last changes fastest.
Arguments:
- token_ids: int32 [8192], P(('dp', 'fsdp')), may hold values from 0 to 31999
- seq_lengths: int32 [32, 8], P(('dp', 'fsdp')), may hold values from 0 to 256, as said below
- noise: bfloat16 [8192, 256], P(('dp', 'fsdp')), may hold values from -6 to 6
- noise_level: float32 [8192], P(('dp', 'fsdp')), may hold values from 0.2 to 2
- table: bfloat16 [32000, 256], P('fsdp'), may hold values from -6 to 6
- w_in: bfloat16 [256, 1024], P('fsdp'), may hold values from -0.375 to 0.375
- b_in: bfloat16 [1024], P('fsdp'), may hold values from -3 to 3
- gain_first: bfloat16 [1024], P('fsdp'), may hold values from 0.25 to 1.75
- shift_first: bfloat16 [1024], P('fsdp'), may hold values from -3 to 3
- w_qkv: bfloat16 [1024, 3072], P('fsdp'), may hold values from -0.1875 to 0.1875
- w_out: bfloat16 [1024, 1024], P('fsdp'), may hold values from -0.75 to 0.75
- b_out: bfloat16 [1024], P('fsdp'), may hold values from -3 to 3
- gain_second: bfloat16 [1024], P('fsdp'), may hold values from 0.25 to 1.75
- shift_second: bfloat16 [1024], P('fsdp'), may hold values from -3 to 3
- w_up: bfloat16 [1024, 4096], P('fsdp'), may hold values from -0.1875 to 0.1875
- b_up: bfloat16 [4096], P('fsdp'), may hold values from -3 to 3
- w_down: bfloat16 [4096, 1024], P('fsdp'), may hold values from -0.09375 to 0.09375
- b_down: bfloat16 [1024], P('fsdp'), may hold values from -3 to 3
- cotangent: bfloat16 [8192, 1024], P(('dp', 'fsdp')), may hold values from -6 to 6
Outputs:
- activations: bfloat16 [8192, 1024], P(('dp', 'fsdp'))
- noise_grad: float32 [8192, 256], P(('dp', 'fsdp'))
- table_grad: float32 [32000, 256], P('fsdp')
- w_in_grad: float32 [256, 1024], P('fsdp')
- b_in_grad: float32 [1024], P('fsdp')
- gain_first_grad: float32 [1024], P('fsdp')
- shift_first_grad: float32 [1024], P('fsdp')
- w_qkv_grad: float32 [1024, 3072], P('fsdp')
- w_out_grad: float32 [1024, 1024], P('fsdp')
- b_out_grad: float32 [1024], P('fsdp')
- gain_second_grad: float32 [1024], P('fsdp')
- shift_second_grad: float32 [1024], P('fsdp')
- w_up_grad: float32 [1024, 4096], P('fsdp')
- b_up_grad: float32 [4096], P('fsdp')
- w_down_grad: float32 [4096, 1024], P('fsdp')
- b_down_grad: float32 [1024], P('fsdp')
Inputs may be any that keep to these rules, and one draw needn't show every extreme that they name: `seq_lengths`: each length is a multiple of 8, a row's lengths sum to 64 or more and to 256 at most; in every draw some row holds one sequence of exactly 256 tokens; slots may be empty.
All inputs are finite; a program needn't handle non-finite values.
Results may differ from a plain program's by a relative error of at most 0.014.
Values may be sent and summed in bfloat16 or wider, within the bound.
A program may use at most 192 MiB of HBM per device.

v0:
```python
import jax
import jax.numpy as jnp
from jax import lax
from jax.sharding import PartitionSpec as P

HEADS = 16
VOCAB = 32000


norm_eps = 1e-05


def standardize(resid):
    centred = resid - jnp.mean(resid, axis=-1, keepdims=True)
    spread = jnp.mean(centred * centred, axis=-1, keepdims=True)
    return centred * lax.rsqrt(spread + norm_eps)


def row_normalize(tok_rows):
    return tok_rows * lax.rsqrt(jnp.mean(tok_rows * tok_rows, axis=1, keepdims=True) + norm_eps)


def exact_gelu(pre_act):
    return jax.nn.gelu(pre_act, approximate=False)


def split_heads(projected):
    tok_count = projected.shape[0]
    width = projected.shape[1] // 3
    head_size = width // HEADS
    key_heads = projected[:, width : 2 * width].reshape(tok_count, HEADS, head_size)
    value_heads = projected[:, 2 * width :].reshape(tok_count, HEADS, head_size)
    row_block = min(512, tok_count)
    query_blocks = projected[:, :width].reshape(tok_count // row_block, row_block, HEADS, head_size)
    return (query_blocks, key_heads, value_heads, row_block)


def block_scores(query_block, key_heads, seg_block, segment):
    raw_scores = (
        jnp.einsum("qhd,khd->hqk", query_block, key_heads, preferred_element_type=jnp.float32)
        * 0.125
    )
    same_seq = seg_block[:, None] == segment[None, :]
    return jnp.where(same_seq[None, :, :], raw_scores, -1000000000.0)


def attention_forward(projected, segment):
    query_blocks, key_heads, value_heads, row_block = split_heads(projected)
    seg_blocks = segment.reshape(-1, row_block)

    def block_step(items_in):
        query_block, seg_block = items_in
        scores = block_scores(query_block, key_heads, seg_block, segment)
        row_max = jnp.max(scores, axis=-1, keepdims=True)
        exp_scores = jnp.exp(scores - row_max)
        row_total = jnp.sum(exp_scores, axis=-1, keepdims=True)
        soft_probs = (exp_scores / row_total).astype(jnp.bfloat16)
        attended = jnp.einsum(
            "hqk,khd->qhd", soft_probs, value_heads, preferred_element_type=jnp.float32
        )
        return (attended, (row_max + jnp.log(row_total))[:, :, 0])

    attended, log_total = lax.map(block_step, (query_blocks, seg_blocks))
    return (attended.reshape(projected.shape[0], -1), log_total)


def attention_backward(projected, segment, log_total, grad_attended):
    query_blocks, key_heads, value_heads, row_block = split_heads(projected)
    seg_blocks = segment.reshape(-1, row_block)
    grad_blocks = grad_attended.reshape(query_blocks.shape)

    def block_step(totals, items_in):
        grad_keys, grad_values = totals
        query_block, seg_block, log_block, grad_block = items_in
        scores = block_scores(query_block, key_heads, seg_block, segment)
        soft_probs = jnp.exp(scores - log_block[:, :, None])
        grad_values = grad_values + jnp.einsum(
            "hqk,qhd->khd",
            soft_probs.astype(jnp.bfloat16),
            grad_block,
            preferred_element_type=jnp.float32,
        )
        grad_probs = jnp.einsum(
            "qhd,khd->hqk", grad_block, value_heads, preferred_element_type=jnp.float32
        )
        grad_scores = soft_probs * (
            grad_probs - jnp.sum(grad_probs * soft_probs, axis=-1, keepdims=True)
        )
        scaled_grad = (grad_scores * 0.125).astype(jnp.bfloat16)
        grad_query = jnp.einsum(
            "hqk,khd->qhd", scaled_grad, key_heads, preferred_element_type=jnp.float32
        )
        grad_keys = grad_keys + jnp.einsum(
            "hqk,qhd->khd", scaled_grad, query_block, preferred_element_type=jnp.float32
        )
        return ((grad_keys, grad_values), grad_query.astype(jnp.bfloat16))

    zero_heads = jnp.zeros(key_heads.shape, jnp.float32)
    (grad_keys, grad_values), grad_queries = lax.scan(
        block_step, (zero_heads, zero_heads), (query_blocks, seg_blocks, log_total, grad_blocks)
    )
    tok_count = projected.shape[0]
    return jnp.concatenate(
        [
            grad_queries.reshape(tok_count, -1),
            grad_keys.astype(jnp.bfloat16).reshape(tok_count, -1),
            grad_values.astype(jnp.bfloat16).reshape(tok_count, -1),
        ],
        axis=1,
    )


def shards(
    token_ids,
    seq_lengths,
    noise,
    noise_level,
    table,
    w_in,
    b_in,
    gain_first,
    shift_first,
    w_qkv,
    w_out,
    b_out,
    gain_second,
    shift_second,
    w_up,
    b_up,
    w_down,
    b_down,
    cotangent,
):
    tok_count = token_ids.shape[0]
    gathered = (
        lax.all_gather(table, "fsdp", axis=0, tiled=True),
        lax.all_gather(w_in, "fsdp", axis=0, tiled=True),
        lax.all_gather(b_in, "fsdp", axis=0, tiled=True),
        lax.all_gather(gain_first, "fsdp", axis=0, tiled=True),
        lax.all_gather(shift_first, "fsdp", axis=0, tiled=True),
        lax.all_gather(w_qkv, "fsdp", axis=0, tiled=True),
        lax.all_gather(w_out, "fsdp", axis=0, tiled=True),
        lax.all_gather(b_out, "fsdp", axis=0, tiled=True),
        lax.all_gather(gain_second, "fsdp", axis=0, tiled=True),
        lax.all_gather(shift_second, "fsdp", axis=0, tiled=True),
        lax.all_gather(w_up, "fsdp", axis=0, tiled=True),
        lax.all_gather(b_up, "fsdp", axis=0, tiled=True),
        lax.all_gather(w_down, "fsdp", axis=0, tiled=True),
        lax.all_gather(b_down, "fsdp", axis=0, tiled=True),
    )
    (
        table_all,
        w_in_all,
        b_in_all,
        gain_first_all,
        shift_first_all,
        w_qkv_all,
        w_out_all,
        b_out_all,
        gain_second_all,
        shift_second_all,
        w_up_all,
        b_up_all,
        w_down_all,
        b_down_all,
    ) = gathered
    seq_ends = jnp.cumsum(seq_lengths[0], dtype=jnp.int32)
    positions = jnp.arange(tok_count, dtype=jnp.int32)
    segment = jnp.sum((positions[:, None] >= seq_ends[None, :]).astype(jnp.int32), axis=1)
    live_rows = (segment < seq_lengths.shape[1]).astype(jnp.float32)[:, None]
    tok_rows = jnp.take(table_all, token_ids, axis=0).astype(jnp.float32)
    embedded = row_normalize(tok_rows)
    scale_in = lax.rsqrt(1.0 + noise_level * noise_level)[:, None]
    scaled = ((embedded + noise_level[:, None] * noise.astype(jnp.float32)) * scale_in).astype(
        jnp.bfloat16
    )
    resid_in = jnp.dot(scaled, w_in_all, preferred_element_type=jnp.float32) + b_in_all.astype(
        jnp.float32
    )
    std_first, first_pull = jax.vjp(standardize, resid_in)
    normed_a = (
        std_first * gain_first_all.astype(jnp.float32) + shift_first_all.astype(jnp.float32)
    ).astype(jnp.bfloat16)
    projected = jnp.dot(normed_a, w_qkv_all, preferred_element_type=jnp.float32).astype(
        jnp.bfloat16
    )
    attended, log_total = attention_forward(projected, segment)
    attended = attended.astype(jnp.bfloat16)
    resid_mid = (
        resid_in
        + jnp.dot(attended, w_out_all, preferred_element_type=jnp.float32)
        + b_out_all.astype(jnp.float32)
    )
    std_second, second_pull = jax.vjp(standardize, resid_mid)
    normed_b = (
        std_second * gain_second_all.astype(jnp.float32) + shift_second_all.astype(jnp.float32)
    ).astype(jnp.bfloat16)
    pre_act = jnp.dot(normed_b, w_up_all, preferred_element_type=jnp.float32) + b_up_all.astype(
        jnp.float32
    )
    activated, gelu_pull = jax.vjp(exact_gelu, pre_act)
    hidden = activated.astype(jnp.bfloat16)
    resid_out = (
        resid_mid
        + jnp.dot(hidden, w_down_all, preferred_element_type=jnp.float32)
        + b_down_all.astype(jnp.float32)
    )
    activations = (resid_out * live_rows).astype(jnp.bfloat16)
    w_in_b, gain_first_b, w_qkv_b, w_out_b, gain_second_b, w_up_b, w_down_b = (
        lax.all_gather(w_in, "fsdp", axis=0, tiled=True),
        lax.all_gather(gain_first, "fsdp", axis=0, tiled=True),
        lax.all_gather(w_qkv, "fsdp", axis=0, tiled=True),
        lax.all_gather(w_out, "fsdp", axis=0, tiled=True),
        lax.all_gather(gain_second, "fsdp", axis=0, tiled=True),
        lax.all_gather(w_up, "fsdp", axis=0, tiled=True),
        lax.all_gather(w_down, "fsdp", axis=0, tiled=True),
    )
    grad_out = cotangent.astype(jnp.float32) * live_rows
    grad_down = grad_out.astype(jnp.bfloat16)
    b_down_term = jnp.sum(grad_down.astype(jnp.float32), axis=0)
    w_down_term = jnp.einsum("tf,td->fd", hidden, grad_down, preferred_element_type=jnp.float32)
    grad_hidden = jnp.einsum("td,fd->tf", grad_down, w_down_b, preferred_element_type=jnp.float32)
    grad_act = gelu_pull(grad_hidden)[0].astype(jnp.bfloat16)
    b_up_term = jnp.sum(grad_act.astype(jnp.float32), axis=0)
    w_up_term = jnp.einsum("td,tf->df", normed_b, grad_act, preferred_element_type=jnp.float32)
    grad_nb = jnp.einsum("tf,df->td", grad_act, w_up_b, preferred_element_type=jnp.float32)
    gain_second_term = jnp.sum(grad_nb * std_second, axis=0)
    shift_second_term = jnp.sum(grad_nb, axis=0)
    grad_mid = grad_out + second_pull(grad_nb * gain_second_b.astype(jnp.float32))[0]
    grad_att = grad_mid.astype(jnp.bfloat16)
    b_out_term = jnp.sum(grad_att.astype(jnp.float32), axis=0)
    w_out_term = jnp.einsum("tc,td->cd", attended, grad_att, preferred_element_type=jnp.float32)
    grad_attended = jnp.einsum(
        "td,cd->tc", grad_att, w_out_b, preferred_element_type=jnp.float32
    ).astype(jnp.bfloat16)
    grad_proj = attention_backward(projected, segment, log_total, grad_attended)
    w_qkv_term = jnp.einsum("td,te->de", normed_a, grad_proj, preferred_element_type=jnp.float32)
    grad_na = jnp.einsum("te,de->td", grad_proj, w_qkv_b, preferred_element_type=jnp.float32)
    gain_first_term = jnp.sum(grad_na * std_first, axis=0)
    shift_first_term = jnp.sum(grad_na, axis=0)
    grad_in = grad_mid + first_pull(grad_na * gain_first_b.astype(jnp.float32))[0]
    grad_pin = grad_in.astype(jnp.bfloat16)
    b_in_term = jnp.sum(grad_pin.astype(jnp.float32), axis=0)
    w_in_term = jnp.einsum("te,td->ed", scaled, grad_pin, preferred_element_type=jnp.float32)
    grad_scaled = jnp.einsum("td,ed->te", grad_pin, w_in_b, preferred_element_type=jnp.float32)
    noise_grad = grad_scaled * noise_level[:, None] * scale_in
    grad_embedded = grad_scaled * scale_in
    (
        w_in_part,
        b_in_part,
        gain_first_part,
        shift_first_part,
        w_qkv_part,
        w_out_part,
        b_out_part,
        gain_second_part,
        shift_second_part,
        w_up_part,
        b_up_part,
        w_down_part,
        b_down_part,
    ) = (
        lax.psum_scatter(w_in_term, "fsdp", scatter_dimension=0, tiled=True),
        lax.psum_scatter(b_in_term, "fsdp", scatter_dimension=0, tiled=True),
        lax.psum_scatter(gain_first_term, "fsdp", scatter_dimension=0, tiled=True),
        lax.psum_scatter(shift_first_term, "fsdp", scatter_dimension=0, tiled=True),
        lax.psum_scatter(w_qkv_term, "fsdp", scatter_dimension=0, tiled=True),
        lax.psum_scatter(w_out_term, "fsdp", scatter_dimension=0, tiled=True),
        lax.psum_scatter(b_out_term, "fsdp", scatter_dimension=0, tiled=True),
        lax.psum_scatter(gain_second_term, "fsdp", scatter_dimension=0, tiled=True),
        lax.psum_scatter(shift_second_term, "fsdp", scatter_dimension=0, tiled=True),
        lax.psum_scatter(w_up_term, "fsdp", scatter_dimension=0, tiled=True),
        lax.psum_scatter(b_up_term, "fsdp", scatter_dimension=0, tiled=True),
        lax.psum_scatter(w_down_term, "fsdp", scatter_dimension=0, tiled=True),
        lax.psum_scatter(b_down_term, "fsdp", scatter_dimension=0, tiled=True),
    )
    dense_grad = jax.ops.segment_sum(grad_embedded, token_ids, num_segments=VOCAB)
    row_grad = lax.psum_scatter(dense_grad, "fsdp", scatter_dimension=0, tiled=True)
    own_table = table.astype(jnp.float32)
    unused_rows, table_pull = jax.vjp(row_normalize, own_table)
    table_part = table_pull(row_grad)[0]
    halves = (
        lax.psum_scatter(
            table_part.astype(jnp.bfloat16), "dp", scatter_dimension=0, tiled=True
        ).astype(jnp.float32),
        lax.psum_scatter(
            w_in_part.astype(jnp.bfloat16), "dp", scatter_dimension=0, tiled=True
        ).astype(jnp.float32),
        lax.psum_scatter(
            b_in_part.astype(jnp.bfloat16), "dp", scatter_dimension=0, tiled=True
        ).astype(jnp.float32),
        lax.psum_scatter(
            gain_first_part.astype(jnp.bfloat16), "dp", scatter_dimension=0, tiled=True
        ).astype(jnp.float32),
        lax.psum_scatter(
            shift_first_part.astype(jnp.bfloat16), "dp", scatter_dimension=0, tiled=True
        ).astype(jnp.float32),
        lax.psum_scatter(
            w_qkv_part.astype(jnp.bfloat16), "dp", scatter_dimension=0, tiled=True
        ).astype(jnp.float32),
        lax.psum_scatter(
            w_out_part.astype(jnp.bfloat16), "dp", scatter_dimension=0, tiled=True
        ).astype(jnp.float32),
        lax.psum_scatter(
            b_out_part.astype(jnp.bfloat16), "dp", scatter_dimension=0, tiled=True
        ).astype(jnp.float32),
        lax.psum_scatter(
            gain_second_part.astype(jnp.bfloat16), "dp", scatter_dimension=0, tiled=True
        ).astype(jnp.float32),
        lax.psum_scatter(
            shift_second_part.astype(jnp.bfloat16), "dp", scatter_dimension=0, tiled=True
        ).astype(jnp.float32),
        lax.psum_scatter(
            w_up_part.astype(jnp.bfloat16), "dp", scatter_dimension=0, tiled=True
        ).astype(jnp.float32),
        lax.psum_scatter(
            b_up_part.astype(jnp.bfloat16), "dp", scatter_dimension=0, tiled=True
        ).astype(jnp.float32),
        lax.psum_scatter(
            w_down_part.astype(jnp.bfloat16), "dp", scatter_dimension=0, tiled=True
        ).astype(jnp.float32),
        lax.psum_scatter(
            b_down_part.astype(jnp.bfloat16), "dp", scatter_dimension=0, tiled=True
        ).astype(jnp.float32),
    )
    summed = (
        lax.all_gather(halves[0].astype(jnp.bfloat16), "dp", axis=0, tiled=True).astype(
            jnp.float32
        ),
        lax.all_gather(halves[1].astype(jnp.bfloat16), "dp", axis=0, tiled=True).astype(
            jnp.float32
        ),
        lax.all_gather(halves[2].astype(jnp.bfloat16), "dp", axis=0, tiled=True).astype(
            jnp.float32
        ),
        lax.all_gather(halves[3].astype(jnp.bfloat16), "dp", axis=0, tiled=True).astype(
            jnp.float32
        ),
        lax.all_gather(halves[4].astype(jnp.bfloat16), "dp", axis=0, tiled=True).astype(
            jnp.float32
        ),
        lax.all_gather(halves[5].astype(jnp.bfloat16), "dp", axis=0, tiled=True).astype(
            jnp.float32
        ),
        lax.all_gather(halves[6].astype(jnp.bfloat16), "dp", axis=0, tiled=True).astype(
            jnp.float32
        ),
        lax.all_gather(halves[7].astype(jnp.bfloat16), "dp", axis=0, tiled=True).astype(
            jnp.float32
        ),
        lax.all_gather(halves[8].astype(jnp.bfloat16), "dp", axis=0, tiled=True).astype(
            jnp.float32
        ),
        lax.all_gather(halves[9].astype(jnp.bfloat16), "dp", axis=0, tiled=True).astype(
            jnp.float32
        ),
        lax.all_gather(halves[10].astype(jnp.bfloat16), "dp", axis=0, tiled=True).astype(
            jnp.float32
        ),
        lax.all_gather(halves[11].astype(jnp.bfloat16), "dp", axis=0, tiled=True).astype(
            jnp.float32
        ),
        lax.all_gather(halves[12].astype(jnp.bfloat16), "dp", axis=0, tiled=True).astype(
            jnp.float32
        ),
        lax.all_gather(halves[13].astype(jnp.bfloat16), "dp", axis=0, tiled=True).astype(
            jnp.float32
        ),
    )
    return (
        activations,
        noise_grad,
        summed[0],
        summed[1],
        summed[2],
        summed[3],
        summed[4],
        summed[5],
        summed[6],
        summed[7],
        summed[8],
        summed[9],
        summed[10],
        summed[11],
        summed[12],
        summed[13],
    )


def solution(mesh):
    in_specs = (
        P(("dp", "fsdp")),
        P(("dp", "fsdp"), None),
        P(("dp", "fsdp"), None),
        P(("dp", "fsdp")),
        P("fsdp", None),
        P("fsdp", None),
        P("fsdp"),
        P("fsdp"),
        P("fsdp"),
        P("fsdp", None),
        P("fsdp", None),
        P("fsdp"),
        P("fsdp"),
        P("fsdp"),
        P("fsdp", None),
        P("fsdp"),
        P("fsdp", None),
        P("fsdp"),
        P(("dp", "fsdp"), None),
    )
    out_specs = (
        P(("dp", "fsdp"), None),
        P(("dp", "fsdp"), None),
        P("fsdp", None),
        P("fsdp", None),
        P("fsdp"),
        P("fsdp"),
        P("fsdp"),
        P("fsdp", None),
        P("fsdp", None),
        P("fsdp"),
        P("fsdp"),
        P("fsdp"),
        P("fsdp", None),
        P("fsdp"),
        P("fsdp", None),
        P("fsdp"),
    )
    return jax.shard_map(shards, mesh=mesh, in_specs=in_specs, out_specs=out_specs, check_vma=False)
```

profile of v0, /device:TPU:15, one launch (start us, length us, event | category | flops | bytes accessed | tf_op | source)
XLA Modules:
  0.0 1547.3 jit_solution(3570104872700256207)
XLA Ops:
  19.2 46.2 %all-reduce.31 = (bf16[1024]{0:T(1024)(128)(2,1)S(1)}, bf16[1024]{0:T(1024)(128)(2,1)S(1)}, bf16[1024]{0:T(1024)(128)(2,1)S(1)}, bf16[1024]{0:T(1024)(128)(2,1)S...) all-reduce(bf16[1024]{0:T(1024)(128)(2,1)S(1)} %dynamic-update-slic, ...), channel_id=1, replica_groups=mesh['dp'=2,'fsdp'=16] {'fsdp'}, use_global_device_ids=true, to_apply=%add | all-reduce | flops 7168 | bytes 28672
  65.4 32.8 %all-gather = bf16[16,1,256]{2,1,0:T(2,128)(2,1)S(1)} all-gather(bf16[1,1,256]{2,1,0:T(2,128)(2,1)S(1)} %reshape.288), channel_id=1, replica_groups=mesh['dp'=2,'fsdp'=16] {'fsdp'}, dimensions={0}, use_global_device_ids=true | all-gather | bytes 8704 | tf_op jit(solution)/shard_map/all_gather | solution.py:147
  101.4 20.5 %all_gather.92 = bf16[256,1024]{1,0:T(8,128)(2,1)S(1)} all-gather(bf16[16,1024]{1,0:T(8,128)(2,1)} %param.24), channel_id=1, replica_groups=mesh['dp'=2,'fsdp'=16] {'fsdp'}, dimensions={0}, use_global_device_ids=true | all-gather | bytes 557056 | tf_op jit(solution)/shard_map/all_gather | solution.py:137
  121.9 15.3 all-gather.8.cloned.1.call-done
  137.2 8.7 gather_fusion
  146.9 54.7 %all-gather.10.cloned.1.call-done = bf16[1024,3072]{1,0:T(8,128)(2,1)} async-done(((bf16[64,3072]{1,0:T(8,128)(2,1)}), bf16[1024,3072]{1,0:T(8,128)(2,1)}) %all-gather.10.cloned.1.call-update) | async-done | bytes 6291472 | tf_op jit(solution)/shard_map/all_gather | solution.py:141
  201.6 4.7 convolution_convert_fusion
  207.8 2.1 fusion.84
  212.7 30.1 %all-gather.12.cloned.1.call-done = bf16[1024,1024]{1,0:T(8,128)(2,1)} async-done(((bf16[64,1024]{1,0:T(8,128)(2,1)}), bf16[1024,1024]{1,0:T(8,128)(2,1)}) %all-gather.12.cloned.1.call-update) | async-done | bytes 2097168 | tf_op jit(solution)/shard_map/all_gather | solution.py:142
  242.8 2.4 fusion.85
  245.5 73.4 %all-gather.14.cloned.1.call-done = bf16[1024,4096]{1,0:T(8,128)(2,1)} async-done(((bf16[64,4096]{1,0:T(8,128)(2,1)}), bf16[1024,4096]{1,0:T(8,128)(2,1)}) %all-gather.14.cloned.1.call-update) | async-done | bytes 8388624 | tf_op jit(solution)/shard_map/all_gather | solution.py:146
  318.9 16.6 %multiply_convert_fusion.1 = (bf16[256,4096]{1,0:T(8,128)(2,1)}, f32[256,4096]{1,0:T(8,128)}, f32[256,4096]{1,0:T(8,128)}) fusion(f32[4096]{0:T(1024)S(1)} %bitcast.70, bf16[1024,4096]{1,0:T(8,128)(2,1)} %all-gather.14.cloned.1.call-done, f32[256,1024]{1,0:T(8,128)S(1)} %get-tuple-element.136, f32[1024]{0:T(1024)S(1)} %convert_element_type.260, ...), kind=kOutput, calls=%fused_computation.14 | convolution fusion | flops 2218000384 | bytes 19949568 | tf_op jit(solution)/shard_map/dot_general | solution.py:198
  335.5 58.6 %all-gather.16.cloned.1.call-done = bf16[4096,1024]{1,0:T(8,128)(2,1)} async-done(((bf16[256,1024]{1,0:T(8,128)(2,1)}), bf16[4096,1024]{1,0:T(8,128)(2,1)}) %all-gather.16.cloned.1.call-update) | async-done | bytes 8388624 | tf_op jit(solution)/shard_map/all_gather | solution.py:148
  394.1 11.9 convert_reduce_fusion
  406.0 2.7 multiply_reduce_fusion.1
  411.8 2.0 copy.67
  413.9 4.1 fusion.86
  419.5 8.5 fusion.41
  428.1 8.6 fusion.44
  436.7 5.4 multiply_reduce_fusion.2
  445.5 3.9 fusion.87
  450.6 7.7 fusion.48
  459.8 8.3 fusion.75
  469.1 9.8 fusion.66
  481.2 15.4 scatter_custom_fusion
  496.7 3.4 reduce-scatter.17.cloned.1.call-done
  501.6 74.2 %reduce-scatter.25.cloned.1.call-done = f32[64,1024]{1,0:T(8,128)} async-done(((f32[1024,1024]{1,0:T(8,128)}), f32[64,1024]{1,0:T(8,128)}) %reduce-scatter.25.cloned.1.call-update) | async-done | bytes 262160 | tf_op jit(solution)/shard_map/reduce_scatter | solution.py:268
  575.8 1.6 convert_element_type.295
  577.5 137.4 %reduce-scatter.21.cloned.1.call-done = f32[64,3072]{1,0:T(8,128)} async-done(((f32[1024,3072]{1,0:T(8,128)}), f32[64,3072]{1,0:T(8,128)}) %reduce-scatter.21.cloned.1.call-update) | async-done | bytes 786448 | tf_op jit(solution)/shard_map/reduce_scatter | solution.py:267
  714.8 1.9 convert_element_type.293
  716.8 179.3 %reduce-scatter.29.cloned.1.call-done = f32[64,4096]{1,0:T(8,128)} async-done(((f32[1024,4096]{1,0:T(8,128)}), f32[64,4096]{1,0:T(8,128)}) %reduce-scatter.29.cloned.1.call-update) | async-done | bytes 1048592 | tf_op jit(solution)/shard_map/reduce_scatter | solution.py:272
  896.1 2.1 convert_element_type.304
  898.2 179.4 %reduce-scatter.33.cloned.1.call-done = f32[256,1024]{1,0:T(8,128)} async-done(((f32[4096,1024]{1,0:T(8,128)}), f32[256,1024]{1,0:T(8,128)}) %reduce-scatter.33.cloned.1.call-update) | async-done | bytes 1048592 | tf_op jit(solution)/shard_map/reduce_scatter | solution.py:274
  1077.7 2.1 convert_element_type.309
  1079.8 329.1 %reduce-scatter.13.cloned.1.call-done = f32[2000,256]{1,0:T(8,128)} async-done(((f32[32000,256]{1,0:T(8,128)}), f32[2000,256]{1,0:T(8,128)}) %reduce-scatter.13.cloned.1.call-update) | async-done | bytes 2048016 | tf_op jit(solution)/shard_map/reduce_scatter | solution.py:278
  1408.9 2.3 fusion.30
  1411.3 1.9 fusion.32
  1416.5 45.0 %all-reduce.30 = (bf16[1024]{0:T(1024)(128)(2,1)S(1)}, bf16[1024]{0:T(1024)(128)(2,1)S(1)}, bf16[1024]{0:T(1024)(128)(2,1)S(1)}, bf16[1024]{0:T(1024)(128)(2,1)S...) all-reduce(f32[1024]{0:T(1024)S(1)} %get-tuple-element.113, ...), channel_id=6, replica_groups=mesh['dp'=2,'fsdp'=16] {'fsdp'}, use_global_device_ids=true, to_apply=%region_22.23.clone | all-reduce | flops 11264 | bytes 67584
  1462.0 4.2 all-reduce.33
  1468.4 3.8 all-reduce.32
  1475.3 3.5 all-gather.1
  1479.8 7.2 fusion.36
  1487.0 3.5 all_gather.106
  1491.2 5.1 all_gather.111
  1496.9 10.7 all_gather.110
  1508.6 7.7 all_gather.115
  1517.3 8.9 all_gather.117
  1527.3 11.6 all_gather.105
  (202 shorter events, 48.5 us)
Async XLA Ops:
  7.2 138.9 %copy-start.23 = (f32[256]{0:T(256)S(1)}, f32[256]{0:T(256)}, u32[]{:S(2)}) copy-start(f32[256]{0:T(256)} %param.22) | copy-start | bytes 3076
  7.2 138.9 %copy-start.22 = (bf16[256,256]{1,0:T(8,128)(2,1)S(1)}, bf16[256,256]{1,0:T(8,128)(2,1)}, u32[]{:S(2)}) copy-start(bf16[256,256]{1,0:T(8,128)(2,1)} %param.21) | copy-start | bytes 393220
  7.2 130.0 %all-gather.8.cloned.1.call-start = ((), (), s32[]{:S(2)}) async-start(), calls=%async_computation.12 | async-start | bytes 17408000 | tf_op jit(solution)/shard_map/all_gather | solution.py:136
  7.9 193.6 %all-gather.10.cloned.1.call-start = ((), (), s32[]{:S(2)}) async-start(), calls=%async_computation.13 | async-start | bytes 6684672 | tf_op jit(solution)/shard_map/all_gather | solution.py:141
  8.7 234.1 %all-gather.12.cloned.1.call-start = ((), (), s32[]{:S(2)}) async-start(), calls=%async_computation.14 | async-start | bytes 2228224 | tf_op jit(solution)/shard_map/all_gather | solution.py:142
  9.4 309.5 %all-gather.14.cloned.1.call-start = ((), (), s32[]{:S(2)}) async-start(), calls=%async_computation.15 | async-start | bytes 8912896 | tf_op jit(solution)/shard_map/all_gather | solution.py:146
  10.0 384.1 %all-gather.16.cloned.1.call-start = ((), (), s32[]{:S(2)}) async-start(), calls=%async_computation.16 | async-start | bytes 8912896 | tf_op jit(solution)/shard_map/all_gather | solution.py:148
  10.6 489.4 %reduce-scatter.17.cloned.1.call-start = ((), (), s32[]{:S(2)}) async-start(), calls=%async_computation.19 | async-start | bytes 1114112 | tf_op jit(solution)/shard_map/reduce_scatter | solution.py:263
  100.6 105.7 %copy-start.24 = (pred[256]{0:T(512)(128)(4,1)}, pred[256]{0:T(512)(128)(4,1)S(1)}, u32[]{:S(2)}) copy-start(pred[256]{0:T(512)(128)(4,1)S(1)} %compare_and_fusion) | copy-start | bytes 772
  121.9 84.4 %copy-start.11 = (bf16[256,1024]{1,0:T(8,128)(2,1)}, bf16[256,1024]{1,0:T(8,128)(2,1)S(1)}, u32[]{:S(2)}) copy-start(bf16[256,1024]{1,0:T(8,128)(2,1)S(1)} %all_gather.92) | copy-start | bytes 1572868
  207.6 2.9 copy-start.18
  207.8 2.7 copy-start.16
  209.9 1.9 copy-start
  212.7 106.2 %copy-start.13 = (bf16[16,64,256]{2,1,0:T(8,128)(2,1)}, bf16[16,64,256]{2,1,0:T(8,128)(2,1)S(1)}, u32[]{:S(2)}) copy-start(bf16[16,64,256]{2,1,0:T(8,128)(2,1)S(1)} %fusion.40) | copy-start | bytes 1572868
  318.9 75.2 %copy-start.4 = (bf16[256,1024]{1,0:T(8,128)(2,1)S(1)}, bf16[256,1024]{1,0:T(8,128)(2,1)}, u32[]{:S(2)}) copy-start(bf16[256,1024]{1,0:T(8,128)(2,1)} %param.37) | copy-start | bytes 1572868
  394.1 11.9 copy-start.27
  406.0 2.7 copy-start.19
  406.0 3.2 copy-start.5
  408.7 1.6 copy-start.17
  409.5 0.8 copy-start.15
  413.9 4.1 copy-start.1
  413.9 4.1 copy-start.10
  436.7 5.9 copy-start.6
  442.1 1.6 copy-start.25
  442.9 0.8 copy-start.8
  445.2 130.6 %reduce-scatter.25.cloned.1.call-start = ((), (), s32[]{:S(2)}) async-start(), calls=%async_computation.23 | async-start | bytes 4456448 | tf_op jit(solution)/shard_map/reduce_scatter | solution.py:268
  449.4 1.0 copy-start.14
  449.4 1.2 copy-start.21
  449.4 265.4 %reduce-scatter.21.cloned.1.call-start = ((), (), s32[]{:S(2)}) async-start(), calls=%async_computation.21 | async-start | bytes 13369344 | tf_op jit(solution)/shard_map/reduce_scatter | solution.py:267
  458.2 1.6 copy-start.20
  458.2 437.8 %reduce-scatter.29.cloned.1.call-start = ((), (), s32[]{:S(2)}) async-start(), calls=%async_computation.25 | async-start | bytes 17825792 | tf_op jit(solution)/shard_map/reduce_scatter | solution.py:272
  468.1 1.0 copy-start.7
  468.1 609.5 %reduce-scatter.33.cloned.1.call-start = ((), (), s32[]{:S(2)}) async-start(), calls=%async_computation.27 | async-start | bytes 17825792 | tf_op jit(solution)/shard_map/reduce_scatter | solution.py:274
  478.9 1.0 copy-start.9
  478.9 1.2 copy-start.12
  479.0 929.9 %reduce-scatter.13.cloned.1.call-start = ((), (), s32[]{:S(2)}) async-start(), calls=%async_computation.17 | async-start | bytes 34816000 | tf_op jit(solution)/shard_map/reduce_scatter | solution.py:278
  496.6 912.3 %copy-start.2 = (bf16[2000,256]{1,0:T(8,128)(2,1)S(1)}, bf16[2000,256]{1,0:T(8,128)(2,1)}, u32[]{:S(2)}) copy-start(bf16[2000,256]{1,0:T(8,128)(2,1)} %param.23) | copy-start | bytes 3072004
  496.6 990.4 %reduce-scatter.19.cloned.1.call-start = ((), (), s32[]{:S(2)}) async-start(), calls=%async_computation.20 | async-start | bytes 49152 | tf_op jit(solution)/shard_map/reduce_scatter | solution.py:286
  501.5 989.6 %reduce-scatter.27.cloned.1.call-start = ((), (), s32[]{:S(2)}) async-start(), calls=%async_computation.24 | async-start | bytes 196608 | tf_op jit(solution)/shard_map/reduce_scatter | solution.py:301
  577.4 919.5 %reduce-scatter.23.cloned.1.call-start = ((), (), s32[]{:S(2)}) async-start(), calls=%async_computation.22 | async-start | bytes 589824 | tf_op jit(solution)/shard_map/reduce_scatter | solution.py:298
  716.8 791.8 %reduce-scatter.31.cloned.1.call-start = ((), (), s32[]{:S(2)}) async-start(), calls=%async_computation.26 | async-start | bytes 786432 | tf_op jit(solution)/shard_map/reduce_scatter | solution.py:313
  898.2 619.1 %reduce-scatter.35.cloned.1.call-start = ((), (), s32[]{:S(2)}) async-start(), calls=%async_computation.28 | async-start | bytes 786432 | tf_op jit(solution)/shard_map/reduce_scatter | solution.py:319
  1079.8 336.1 %copy-start.26 = (bf16[1024]{0:T(1024)(128)(2,1)S(1)}, bf16[1024]{0:T(1024)(128)(2,1)}, u32[]{:S(2)}) copy-start(bf16[1024]{0:T(1024)(128)(2,1)} %get-tuple-element.95) | copy-start | bytes 6148
  1079.8 447.5 %reduce-scatter.15.cloned.1.call-start = ((), (), s32[]{:S(2)}) async-start(), calls=%async_computation.18 | async-start | bytes 1536000 | tf_op jit(solution)/shard_map/reduce_scatter | solution.py:283
  1408.9 2.4 copy-start.3
Sparse Core Ops, SparseCore 0:
  10.3 126.8 all-gather.7
  139.5 62.0 all-gather.9
  203.7 39.0 all-gather.11
  244.8 74.0 all-gather.13
  320.9 73.1 all-gather.15
  445.3 54.6 reduce-scatter.16
  504.4 71.3 reduce-scatter.24
  579.8 134.9 reduce-scatter.20
  718.9 177.0 reduce-scatter.28
  900.0 177.5 reduce-scatter.32
  1082.0 326.8 reduce-scatter.12
  1411.6 8.8 reduce-scatter.18
  1423.4 10.6 reduce-scatter.26
  1436.9 13.1 reduce-scatter.22
  1452.7 14.6 reduce-scatter.30
  1469.6 14.5 reduce-scatter.34
  1486.9 23.4 reduce-scatter.14
where the time goes:
time: 1570 us; the launch traced here: 1550 us
  waiting for transfers between devices  1140 us (73%)
  blocking collectives  203 us (13%)
  matrix products  111 us (7%)
  other arithmetic  44.7 us (3%)
  local copies, waits for them, and re-layouts  30.7 us (2%)
  between operations  18.8 us (1%)
    reduce_scatter x1, waiting for transfers between devices, shards(): lax.psum_scatter(dense_grad, 'fsdp', scatter_dimension=0, tiled=True)  329 us
    reduce_scatter x1, waiting for transfers between devices, shards(): lax.psum_scatter(w_down_term, 'fsdp', scatter_dimension=0, tiled=True)  179 us
    reduce_scatter x1, waiting for transfers between devices, shards(): lax.psum_scatter(w_up_term, 'fsdp', scatter_dimension=0, tiled=True)  179 us
    reduce_scatter x1, waiting for transfers between devices, shards(): lax.psum_scatter(w_qkv_term, 'fsdp', scatter_dimension=0, tiled=True)  137 us
    unnamed x4, blocking collectives  99.2 us
    reduce_scatter x1, waiting for transfers between devices, shards(): lax.psum_scatter(w_out_term, 'fsdp', scatter_dimension=0, tiled=True)  74.2 us
    all_gather x1, waiting for transfers between devices, shards(): lax.all_gather(w_up, 'fsdp', axis=0, tiled=True)  73.4 us
    all_gather x1, waiting for transfers between devices, shards(): lax.all_gather(w_down, 'fsdp', axis=0, tiled=True)  58.6 us
  transfers between devices with their start and end apart: 17, of which 11 were waited for; matrix products, arithmetic and copies ran while one was open for 8% of the time, Pallas kernels for 0%

commit v1 on v0

v1 whole, which is shorter than its diff:
```python
import jax
import jax.numpy as jnp
from jax import lax
from jax.sharding import PartitionSpec as P

HEADS = 16
VOCAB = 32000


norm_eps = 1e-05


def standardize(resid):
    centred = resid - jnp.mean(resid, axis=-1, keepdims=True)
    spread = jnp.mean(centred * centred, axis=-1, keepdims=True)
    return centred * lax.rsqrt(spread + norm_eps)


def row_normalize(tok_rows):
    return tok_rows * lax.rsqrt(jnp.mean(tok_rows * tok_rows, axis=1, keepdims=True) + norm_eps)


def exact_gelu(pre_act):
    return jax.nn.gelu(pre_act, approximate=False)


def split_heads(projected):
    tok_count = projected.shape[0]
    width = projected.shape[1] // 3
    head_size = width // HEADS
    key_heads = projected[:, width : 2 * width].reshape(tok_count, HEADS, head_size)
    value_heads = projected[:, 2 * width :].reshape(tok_count, HEADS, head_size)
    row_block = min(512, tok_count)
    query_blocks = projected[:, :width].reshape(tok_count // row_block, row_block, HEADS, head_size)
    return (query_blocks, key_heads, value_heads, row_block)


def block_scores(query_block, key_heads, seg_block, segment):
    raw_scores = (
        jnp.einsum("qhd,khd->hqk", query_block, key_heads, preferred_element_type=jnp.float32)
        * 0.125
    )
    same_seq = seg_block[:, None] == segment[None, :]
    return jnp.where(same_seq[None, :, :], raw_scores, -1000000000.0)


def attention_forward(projected, segment):
    query_blocks, key_heads, value_heads, row_block = split_heads(projected)
    seg_blocks = segment.reshape(-1, row_block)

    def block_step(items_in):
        query_block, seg_block = items_in
        scores = block_scores(query_block, key_heads, seg_block, segment)
        row_max = jnp.max(scores, axis=-1, keepdims=True)
        exp_scores = jnp.exp(scores - row_max)
        row_total = jnp.sum(exp_scores, axis=-1, keepdims=True)
        soft_probs = (exp_scores / row_total).astype(jnp.bfloat16)
        attended = jnp.einsum(
            "hqk,khd->qhd", soft_probs, value_heads, preferred_element_type=jnp.float32
        )
        return (attended, (row_max + jnp.log(row_total))[:, :, 0])

    attended, log_total = lax.map(block_step, (query_blocks, seg_blocks))
    return (attended.reshape(projected.shape[0], -1), log_total)


def attention_backward(projected, segment, log_total, grad_attended):
    query_blocks, key_heads, value_heads, row_block = split_heads(projected)
    seg_blocks = segment.reshape(-1, row_block)
    grad_blocks = grad_attended.reshape(query_blocks.shape)

    def block_step(totals, items_in):
        grad_keys, grad_values = totals
        query_block, seg_block, log_block, grad_block = items_in
        scores = block_scores(query_block, key_heads, seg_block, segment)
        soft_probs = jnp.exp(scores - log_block[:, :, None])
        grad_values = grad_values + jnp.einsum(
            "hqk,qhd->khd",
            soft_probs.astype(jnp.bfloat16),
            grad_block,
            preferred_element_type=jnp.float32,
        )
        grad_probs = jnp.einsum(
            "qhd,khd->hqk", grad_block, value_heads, preferred_element_type=jnp.float32
        )
        grad_scores = soft_probs * (
            grad_probs - jnp.sum(grad_probs * soft_probs, axis=-1, keepdims=True)
        )
        scaled_grad = (grad_scores * 0.125).astype(jnp.bfloat16)
        grad_query = jnp.einsum(
            "hqk,khd->qhd", scaled_grad, key_heads, preferred_element_type=jnp.float32
        )
        grad_keys = grad_keys + jnp.einsum(
            "hqk,qhd->khd", scaled_grad, query_block, preferred_element_type=jnp.float32
        )
        return ((grad_keys, grad_values), grad_query.astype(jnp.bfloat16))

    zero_heads = jnp.zeros(key_heads.shape, jnp.float32)
    (grad_keys, grad_values), grad_queries = lax.scan(
        block_step, (zero_heads, zero_heads), (query_blocks, seg_blocks, log_total, grad_blocks)
    )
    tok_count = projected.shape[0]
    return jnp.concatenate(
        [
            grad_queries.reshape(tok_count, -1),
            grad_keys.astype(jnp.bfloat16).reshape(tok_count, -1),
            grad_values.astype(jnp.bfloat16).reshape(tok_count, -1),
        ],
        axis=1,
    )


def shards(
    token_ids,
    seq_lengths,
    noise,
    noise_level,
    table,
    w_in,
    b_in,
    gain_first,
    shift_first,
    w_qkv,
    w_out,
    b_out,
    gain_second,
    shift_second,
    w_up,
    b_up,
    w_down,
    b_down,
    cotangent,
):
    tok_count = token_ids.shape[0]
    row_count = table.shape[0]
    group_ids = lax.all_gather(token_ids, "fsdp", axis=0, tiled=True)
    first_row = lax.axis_index("fsdp") * row_count
    owned = (group_ids[:, None] == first_row + jnp.arange(row_count)[None, :]).astype(jnp.bfloat16)
    owned_rows = jnp.dot(owned, table, preferred_element_type=jnp.float32).astype(jnp.bfloat16)
    tok_rows = lax.psum_scatter(owned_rows, "fsdp", scatter_dimension=0, tiled=True)
    tok_rows = tok_rows.astype(jnp.float32)
    vectors = (b_in, gain_first, shift_first, b_out, gain_second, shift_second, b_up, b_down)
    vec_all = lax.all_gather(jnp.concatenate(vectors), "fsdp", axis=0, tiled=False)
    vec_at = [0]
    for vector in vectors:
        vec_at.append(vec_at[-1] + vector.shape[0])
    (
        b_in_all,
        gain_first_all,
        shift_first_all,
        b_out_all,
        gain_second_all,
        shift_second_all,
        b_up_all,
        b_down_all,
    ) = [vec_all[:, lo:hi].reshape(-1) for lo, hi in zip(vec_at[:-1], vec_at[1:])]
    w_in_all = lax.all_gather(w_in, "fsdp", axis=0, tiled=True)
    w_qkv_all = lax.all_gather(w_qkv, "fsdp", axis=0, tiled=True)
    w_out_all = lax.all_gather(w_out, "fsdp", axis=0, tiled=True)
    w_up_all = lax.all_gather(w_up, "fsdp", axis=0, tiled=True)
    w_down_all = lax.all_gather(w_down, "fsdp", axis=0, tiled=True)
    seq_ends = jnp.cumsum(seq_lengths[0], dtype=jnp.int32)
    positions = jnp.arange(tok_count, dtype=jnp.int32)
    segment = jnp.sum((positions[:, None] >= seq_ends[None, :]).astype(jnp.int32), axis=1)
    live_rows = (segment < seq_lengths.shape[1]).astype(jnp.float32)[:, None]
    embedded = row_normalize(tok_rows)
    scale_in = lax.rsqrt(1.0 + noise_level * noise_level)[:, None]
    scaled = ((embedded + noise_level[:, None] * noise.astype(jnp.float32)) * scale_in).astype(
        jnp.bfloat16
    )
    resid_in = jnp.dot(scaled, w_in_all, preferred_element_type=jnp.float32) + b_in_all.astype(
        jnp.float32
    )
    std_first, first_pull = jax.vjp(standardize, resid_in)
    normed_a = (
        std_first * gain_first_all.astype(jnp.float32) + shift_first_all.astype(jnp.float32)
    ).astype(jnp.bfloat16)
    projected = jnp.dot(normed_a, w_qkv_all, preferred_element_type=jnp.float32).astype(
        jnp.bfloat16
    )
    attended, log_total = attention_forward(projected, segment)
    attended = attended.astype(jnp.bfloat16)
    resid_mid = (
        resid_in
        + jnp.dot(attended, w_out_all, preferred_element_type=jnp.float32)
        + b_out_all.astype(jnp.float32)
    )
    std_second, second_pull = jax.vjp(standardize, resid_mid)
    normed_b = (
        std_second * gain_second_all.astype(jnp.float32) + shift_second_all.astype(jnp.float32)
    ).astype(jnp.bfloat16)
    pre_act = jnp.dot(normed_b, w_up_all, preferred_element_type=jnp.float32) + b_up_all.astype(
        jnp.float32
    )
    activated, gelu_pull = jax.vjp(exact_gelu, pre_act)
    hidden = activated.astype(jnp.bfloat16)
    resid_out = (
        resid_mid
        + jnp.dot(hidden, w_down_all, preferred_element_type=jnp.float32)
        + b_down_all.astype(jnp.float32)
    )
    activations = (resid_out * live_rows).astype(jnp.bfloat16)
    grad_out = cotangent.astype(jnp.float32) * live_rows
    grad_down = grad_out.astype(jnp.bfloat16)
    b_down_term = jnp.sum(grad_down.astype(jnp.float32), axis=0)
    w_down_term = jnp.einsum("tf,td->fd", hidden, grad_down, preferred_element_type=jnp.float32)
    grad_hidden = jnp.einsum("td,fd->tf", grad_down, w_down_all, preferred_element_type=jnp.float32)
    grad_act = gelu_pull(grad_hidden)[0].astype(jnp.bfloat16)
    b_up_term = jnp.sum(grad_act.astype(jnp.float32), axis=0)
    w_up_term = jnp.einsum("td,tf->df", normed_b, grad_act, preferred_element_type=jnp.float32)
    grad_nb = jnp.einsum("tf,df->td", grad_act, w_up_all, preferred_element_type=jnp.float32)
    gain_second_term = jnp.sum(grad_nb * std_second, axis=0)
    shift_second_term = jnp.sum(grad_nb, axis=0)
    grad_mid = grad_out + second_pull(grad_nb * gain_second_all.astype(jnp.float32))[0]
    grad_att = grad_mid.astype(jnp.bfloat16)
    b_out_term = jnp.sum(grad_att.astype(jnp.float32), axis=0)
    w_out_term = jnp.einsum("tc,td->cd", attended, grad_att, preferred_element_type=jnp.float32)
    grad_attended = jnp.einsum(
        "td,cd->tc", grad_att, w_out_all, preferred_element_type=jnp.float32
    ).astype(jnp.bfloat16)
    grad_proj = attention_backward(projected, segment, log_total, grad_attended)
    w_qkv_term = jnp.einsum("td,te->de", normed_a, grad_proj, preferred_element_type=jnp.float32)
    grad_na = jnp.einsum("te,de->td", grad_proj, w_qkv_all, preferred_element_type=jnp.float32)
    gain_first_term = jnp.sum(grad_na * std_first, axis=0)
    shift_first_term = jnp.sum(grad_na, axis=0)
    grad_in = grad_mid + first_pull(grad_na * gain_first_all.astype(jnp.float32))[0]
    grad_pin = grad_in.astype(jnp.bfloat16)
    b_in_term = jnp.sum(grad_pin.astype(jnp.float32), axis=0)
    w_in_term = jnp.einsum("te,td->ed", scaled, grad_pin, preferred_element_type=jnp.float32)
    grad_scaled = jnp.einsum("td,ed->te", grad_pin, w_in_all, preferred_element_type=jnp.float32)
    noise_grad = grad_scaled * noise_level[:, None] * scale_in
    grad_embedded = grad_scaled * scale_in
    all_ids = lax.all_gather(token_ids, ("dp", "fsdp"), axis=0, tiled=True)
    all_grads = lax.all_gather(
        grad_embedded.astype(jnp.bfloat16), ("dp", "fsdp"), axis=0, tiled=True
    )
    owners = (first_row + jnp.arange(row_count)[:, None] == all_ids[None, :]).astype(jnp.bfloat16)
    row_grad = jnp.dot(owners, all_grads, preferred_element_type=jnp.float32)
    own_table = table.astype(jnp.float32)
    unused_rows, table_pull = jax.vjp(row_normalize, own_table)
    table_part = table_pull(row_grad)[0]

    def reduce_matrix(term):
        part = lax.psum_scatter(
            term.astype(jnp.bfloat16), "fsdp", scatter_dimension=0, tiled=True
        )
        return lax.psum(part, "dp").astype(jnp.float32)

    vec_terms = (
        b_in_term,
        gain_first_term,
        shift_first_term,
        b_out_term,
        gain_second_term,
        shift_second_term,
        b_up_term,
        b_down_term,
    )
    shard_count = lax.axis_size("fsdp")
    vec_term = jnp.concatenate([v.reshape(shard_count, -1) for v in vec_terms], axis=1)
    vec_part = lax.psum(vec_term, ("dp", "fsdp"))
    own_vec = lax.dynamic_index_in_dim(vec_part, lax.axis_index("fsdp"), 0, keepdims=False)
    vec_grads = [own_vec[lo:hi] for lo, hi in zip(vec_at[:-1], vec_at[1:])]
    return (
        activations,
        noise_grad,
        table_part,
        reduce_matrix(w_in_term),
        vec_grads[0],
        vec_grads[1],
        vec_grads[2],
        reduce_matrix(w_qkv_term),
        reduce_matrix(w_out_term),
        vec_grads[3],
        vec_grads[4],
        vec_grads[5],
        reduce_matrix(w_up_term),
        vec_grads[6],
        reduce_matrix(w_down_term),
        vec_grads[7],
    )


def solution(mesh):
    in_specs = (
        P(("dp", "fsdp")),
        P(("dp", "fsdp"), None),
        P(("dp", "fsdp"), None),
        P(("dp", "fsdp")),
        P("fsdp", None),
        P("fsdp", None),
        P("fsdp"),
        P("fsdp"),
        P("fsdp"),
        P("fsdp", None),
        P("fsdp", None),
        P("fsdp"),
        P("fsdp"),
        P("fsdp"),
        P("fsdp", None),
        P("fsdp"),
        P("fsdp", None),
        P("fsdp"),
        P(("dp", "fsdp"), None),
    )
    out_specs = (
        P(("dp", "fsdp"), None),
        P(("dp", "fsdp"), None),
        P("fsdp", None),
        P("fsdp", None),
        P("fsdp"),
        P("fsdp"),
        P("fsdp"),
        P("fsdp", None),
        P("fsdp", None),
        P("fsdp"),
        P("fsdp"),
        P("fsdp"),
        P("fsdp", None),
        P("fsdp"),
        P("fsdp", None),
        P("fsdp"),
    )
    return jax.shard_map(shards, mesh=mesh, in_specs=in_specs, out_specs=out_specs, check_vma=False)
```

time: 1570 us -> 972 us (0.62)
  waiting for transfers between devices: 1140 us -> 607 us
  other arithmetic: 44.7 us -> 14.7 us
  blocking collectives: 203 us -> 183 us
  local copies, waits for them, and re-layouts: 30.7 us -> 13.7 us
  matrix products: 111 us -> 127 us
    reduce_scatter x12 -> x6, waiting for transfers between devices: 903 us -> 303 us  [the longest x5 303 us: reduce_matrix(): lax.psum_scatter(term.astype(jnp.bfloat16), 'fsdp', scatter_dimension=0,...]
    psum x0 -> x2, blocking collectives: none -> 49.7 us  [the longest x1 43.4 us: shards(): vec_part = lax.psum(vec_term, ('dp', 'fsdp'))]
    unnamed x4 -> x1, blocking collectives: 99.2 us -> 49.5 us
    psum x0 -> x1, waiting for transfers between devices: none -> 34.4 us  [reduce_matrix(): return lax.psum(part, 'dp').astype(jnp.float32)]
    all_gather x5, waiting for transfers between devices: 232 us -> 266 us  [the longest x1 73.6 us: shards(): w_up_all = lax.all_gather(w_up, 'fsdp', axis=0, tiled=True)]
    dot_general x5 -> x7, matrix products: 22.6 us -> 46.1 us  [the longest x1 16.1 us: shards(): row_grad = jnp.dot(owners, all_grads, preferred_element_type=jnp.float32)]
    all_gather x9 -> x3, blocking collectives: 104 us -> 83.7 us  [the longest x1 34.8 us: shards(): all_ids = lax.all_gather(token_ids, ('dp', 'fsdp'), axis=0, tiled=True)]
  transfers between devices with their start and end apart: 17 -> 12, of which waited for: 11 -> 9; matrix products, arithmetic and copies ran while one was open for 8% -> 9% of each run, Pallas kernels for 0% -> 0%
where the time goes in v1:
time: 972 us; the launch traced here: 962 us
  waiting for transfers between devices  607 us (62%)
  blocking collectives  183 us (19%)
  matrix products  127 us (13%)
  between operations  15.9 us (2%)
  other arithmetic  14.7 us (2%)
  local copies, waits for them, and re-layouts  13.7 us (1%)
    reduce_scatter x5, waiting for transfers between devices, reduce_matrix(): lax.psum_scatter(term.astype(jnp.bfloat16), 'fsdp', scatter_dimension=0,...  303 us
    all_gather x1, waiting for transfers between devices, shards(): w_up_all = lax.all_gather(w_up, 'fsdp', axis=0, tiled=True)  73.6 us
    all_gather x1, waiting for transfers between devices, shards(): lax.all_gather(grad_embedded.astype(jnp.bfloat16), ('dp', 'fsdp'), axis=0...  64.7 us
    all_gather x1, waiting for transfers between devices, shards(): w_down_all = lax.all_gather(w_down, 'fsdp', axis=0, tiled=True)  59.3 us
    unnamed x1, blocking collectives  49.5 us
    psum x1, blocking collectives, shards(): vec_part = lax.psum(vec_term, ('dp', 'fsdp'))  43.4 us
    all_gather x1, waiting for transfers between devices, shards(): w_qkv_all = lax.all_gather(w_qkv, 'fsdp', axis=0, tiled=True)  38.5 us
    all_gather x1, blocking collectives, shards(): all_ids = lax.all_gather(token_ids, ('dp', 'fsdp'), axis=0, tiled=True)  34.8 us
  transfers between devices with their start and end apart: 12, of which 9 were waited for; matrix products, arithmetic and copies ran while one was open for 9% of the time, Pallas kernels for 0%

profile of v1, /device:TPU:15, one launch (start us, length us, event | category | flops | bytes accessed | tf_op | source)
XLA Modules:
  0.0 962.1 jit_solution(10206184972452892281)
XLA Ops:
  7.2 15.8 %all-gather.1 = s32[16,1,256]{2,1,0:T(1,128)S(1)} all-gather(s32[1,1,256]{2,1,0:T(1,128)} %bitcast.89), channel_id=1, replica_groups=mesh['dp'=2,'fsdp'=16] {'fsdp'}, dimensions={0}, use_global_device_ids=true | all-gather | bytes 17408 | tf_op jit(solution)/shard_map/all_gather | solution.py:136
  23.2 7.5 fusion.9
  35.1 49.5 %all-reduce = bf16[11264]{0:T(1024)(128)(2,1)S(1)} all-reduce(bf16[11264]{0:T(1024)(128)(2,1)S(1)} %dynamic-update-slice), channel_id=2, replica_groups=mesh['dp'=2,'fsdp'=16] {'fsdp'}, use_global_device_ids=true, to_apply=%add | all-reduce | flops 11264 | bytes 45056
  85.7 33.0 %all_gather.31 = bf16[256,1024]{1,0:T(8,128)(2,1)S(1)} all-gather(bf16[16,1024]{1,0:T(8,128)(2,1)S(1)} %copy-done.23), channel_id=1, replica_groups=mesh['dp'=2,'fsdp'=16] {'fsdp'}, dimensions={0}, use_global_device_ids=true | all-gather | bytes 557056 | tf_op jit(solution)/shard_map/all_gather | solution.py:157
  118.7 1.1 fusion.58
  119.9 1.4 fusion.83
  121.5 38.5 %all-gather.9.cloned.1.call-done = bf16[1024,3072]{1,0:T(8,128)(2,1)} async-done(((bf16[64,3072]{1,0:T(8,128)(2,1)}), bf16[1024,3072]{1,0:T(8,128)(2,1)}) %all-gather.9.cloned.1.call-update) | async-done | bytes 6291472 | tf_op jit(solution)/shard_map/all_gather | solution.py:158
  160.0 4.7 convolution_convert_fusion.3
  164.8 1.0 copy.65
  166.3 2.1 fusion.84
  169.0 1.4 copy-done
  171.2 30.2 %all-gather.11.cloned.1.call-done = bf16[1024,1024]{1,0:T(8,128)(2,1)} async-done(((bf16[64,1024]{1,0:T(8,128)(2,1)}), bf16[1024,1024]{1,0:T(8,128)(2,1)}) %all-gather.11.cloned.1.call-update) | async-done | bytes 2097168 | tf_op jit(solution)/shard_map/all_gather | solution.py:159
  201.5 2.4 fusion.85
  204.2 73.6 %all-gather.13.cloned.1.call-done = bf16[1024,4096]{1,0:T(8,128)(2,1)} async-done(((bf16[64,4096]{1,0:T(8,128)(2,1)}), bf16[1024,4096]{1,0:T(8,128)(2,1)}) %all-gather.13.cloned.1.call-update) | async-done | bytes 8388624 | tf_op jit(solution)/shard_map/all_gather | solution.py:160
  277.8 16.1 %multiply_convert_fusion.1 = (bf16[256,4096]{1,0:T(8,128)(2,1)}, f32[256,4096]{1,0:T(8,128)}, f32[256,4096]{1,0:T(8,128)}) fusion(f32[4096]{0:T(1024)S(1)} %bitcast.87, bf16[1024,4096]{1,0:T(8,128)(2,1)} %all-gather.13.cloned.1.call-done, f32[256,1024]{1,0:T(8,128)S(1)} %get-tuple-element.122, f32[1024]{0:T(1024)S(1)} %reshape.336, f32[1024]{0:T(1024)S(1)} %reshape.335, ...), kind=kOutput, calls=%fused_computation.22 | convolution fusion | flops 2218000384 | bytes 19949568 | tf_op jit(solution)/shard_map/dot_general | solution.py:192
  293.9 59.3 %all-gather.15.cloned.1.call-done = bf16[4096,1024]{1,0:T(8,128)(2,1)} async-done(((bf16[256,1024]{1,0:T(8,128)(2,1)}), bf16[4096,1024]{1,0:T(8,128)(2,1)}) %all-gather.15.cloned.1.call-update) | async-done | bytes 8388624 | tf_op jit(solution)/shard_map/all_gather | solution.py:161
  353.2 11.8 %convert_reduce_fusion = (f32[4096]{0:T(1024)S(1)}, bf16[256,4096]{1,0:T(8,128)(2,1)S(1)}) fusion(f32[256,4096]{1,0:T(8,128)} %get-tuple-element.94, f32[256,4096]{1,0:T(8,128)} %get-tuple-element.123, bf16[4096,1024]{1,0:T(8,128)(2,1)} %all-gather.15.cloned.1.call-done, bf16[256,1024]{1,0:T(8,128)(2,1)S(1)} %copy-done.7, f32[256]{0:T(256)S(1)} %compare_convert_fusion), kind=kOutput, calls=%fused_computation.16 | convolution fusion | flops 2165043200 | bytes 19416064 | tf_op jit(solution)/shard_map/td,fd->tf/dot_general | solution.py:207
  365.0 2.7 multiply_reduce_fusion.1
  369.3 1.5 convolution_convert_fusion.6
  370.9 2.0 copy.67
  372.9 4.1 fusion.86
  377.0 1.6 fusion.45
  378.6 8.8 fusion.49
  387.4 8.8 fusion.52
  396.2 5.4 multiply_reduce_fusion.2
  403.2 1.3 convolution_convert_fusion.5
  404.8 3.2 convolution_convert_fusion.4
  408.1 5.8 convolution_convert_fusion.2
  414.0 1.5 copy-done.12
  415.5 5.7 convolution_convert_fusion.1
  421.3 1.0 copy-done.10
  422.3 7.3 convolution_convert_fusion
  430.8 1.1 multiply_convert_fusion.2
  432.0 34.8 %all-gather.2 = s32[32,1,256]{2,1,0:T(1,128)S(1)} all-gather(s32[1,1,256]{2,1,0:T(1,128)S(1)} %bitcast.90), channel_id=1, replica_groups=mesh['dp'=2,'fsdp'=16] {'dp','fsdp'}, dimensions={0}, use_global_device_ids=true | all-gather | bytes 33792 | tf_op jit(solution)/shard_map/all_gather | solution.py:233
  467.4 43.4 %psum.43 = f32[16,704]{1,0:T(8,128)S(1)} all-reduce(f32[16,704]{1,0:T(8,128)S(1)} %concatenate.11), channel_id=1, replica_groups=mesh['dp'=2,'fsdp'=16] {'dp','fsdp'}, use_global_device_ids=true, to_apply=%region_27.28 | all-reduce | flops 11264 | bytes 90112 | tf_op jit(solution)/shard_map/psum | solution.py:261
  512.1 7.3 fusion.44
  519.4 6.3 psum.42
  526.3 86.3 %reduce-scatter.11.cloned.1.call-done = bf16[64,3072]{1,0:T(8,128)(2,1)} async-done(((bf16[1024,3072]{1,0:T(8,128)(2,1)}), bf16[64,3072]{1,0:T(8,128)(2,1)}) %reduce-scatter.11.cloned.1.call-update) | async-done | bytes 393232 | tf_op jit(solution)/shard_map/reduce_scatter | solution.py:244
  612.6 108.7 %reduce-scatter.15.cloned.1.call-done = bf16[64,4096]{1,0:T(8,128)(2,1)} async-done(((bf16[1024,4096]{1,0:T(8,128)(2,1)}), bf16[64,4096]{1,0:T(8,128)(2,1)}) %reduce-scatter.15.cloned.1.call-update) | async-done | bytes 524304 | tf_op jit(solution)/shard_map/reduce_scatter | solution.py:244
  721.3 108.4 %reduce-scatter.17.cloned.1.call-done = bf16[256,1024]{1,0:T(8,128)(2,1)} async-done(((bf16[4096,1024]{1,0:T(8,128)(2,1)}), bf16[256,1024]{1,0:T(8,128)(2,1)}) %reduce-scatter.17.cloned.1.call-update) | async-done | bytes 524304 | tf_op jit(solution)/shard_map/reduce_scatter | solution.py:244
  829.7 64.7 %all-gather.17.cloned.1.call-done = bf16[8192,256]{1,0:T(8,128)(2,1)} async-done(((bf16[256,256]{1,0:T(8,128)(2,1)}), bf16[8192,256]{1,0:T(8,128)(2,1)}) %all-gather.17.cloned.1.call-update) | async-done | bytes 4194320 | tf_op jit(solution)/shard_map/all_gather | solution.py:234
  894.4 16.1 %fusion.39 = (f32[2000]{0:T(1024)S(1)}, f32[2000]{0:T(1024)S(1)}, f32[2000,256]{1,0:T(8,128)S(1)}) fusion(bf16[2000,256]{1,0:T(8,128)(2,1)S(1)} %copy-done.20, bf16[8192,256]{1,0:T(8,128)(2,1)} %all-gather.17.cloned.1.call-done, s32[8192]{0:T(1024)S(1)} %bitcast.86, s32[2000]{0:T(1024)S(1)} %iota_add_fusion), kind=kOutput, calls=%fused_computation.55 | convolution fusion | flops 8407547904 | bytes 7323072 | tf_op jit(solution)/shard_map/dot_general | solution.py:238
  910.5 2.1 add_add_fusion
  912.6 34.4 %all-reduce.4.cloned.1.call-done = (bf16[64,3072]{1,0:T(8,128)(2,1)}, bf16[64,1024]{1,0:T(8,128)(2,1)}, bf16[64,4096]{1,0:T(8,128)(2,1)}, bf16[256,1024]{1,0:T(8,128)(2,1)}) async-done(((bf16[64,3072]{1,0:T(8,128)(2,1)}, bf16[64,1024]{1,0:T(8,128)(2,1)}, bf16[64,4096]{1,0:T(8,128)(2,1)}, bf16[256,1024]{1,0:T(8,128)(2,1)}), (bf16[64,3072]{1,0:T(8,128)(2,1)}, bf16[64,1024]{1,0:T(8,128)(2,1)}, ...) | async-done | bytes 1572880 | tf_op jit(solution)/shard_map/psum | solution.py:247
  947.0 1.6 convert_element_type.283
  948.6 1.9 convert_element_type.281
  950.6 2.1 convert_element_type.285
  952.6 2.1 convert_element_type.287
  (153 shorter events, 14.6 us)
Async XLA Ops:
  7.2 111.5 %reduce-scatter.7.cloned.1.call-start = ((), (), s32[]{:S(2)}) async-start(), calls=%async_computation.6 | async-start | bytes 2228224 | tf_op jit(solution)/shard_map/reduce_scatter | solution.py:140
  23.1 10.4 %copy-start.36 = (u32[32]{0:T(128)S(1)}, u32[32]{0:T(128)}, u32[]{:S(2)}) copy-start(u32[32]{0:T(128)} %constant.151) | copy-start | bytes 388
  23.1 11.6 %copy-start.26 = (bf16[64]{0:T(256)(128)(2,1)S(1)}, bf16[64]{0:T(256)(128)(2,1)}, u32[]{:S(2)}) copy-start(bf16[64]{0:T(256)(128)(2,1)} %param.25) | copy-start | bytes 388
  23.1 11.6 %copy-start.27 = (bf16[64]{0:T(256)(128)(2,1)S(1)}, bf16[64]{0:T(256)(128)(2,1)}, u32[]{:S(2)}) copy-start(bf16[64]{0:T(256)(128)(2,1)} %param.26) | copy-start | bytes 388
  23.1 11.6 %copy-start.28 = (bf16[64]{0:T(256)(128)(2,1)S(1)}, bf16[64]{0:T(256)(128)(2,1)}, u32[]{:S(2)}) copy-start(bf16[64]{0:T(256)(128)(2,1)} %param.27) | copy-start | bytes 388
  23.1 11.6 %copy-start.29 = (bf16[64]{0:T(256)(128)(2,1)S(1)}, bf16[64]{0:T(256)(128)(2,1)}, u32[]{:S(2)}) copy-start(bf16[64]{0:T(256)(128)(2,1)} %param.30) | copy-start | bytes 388
  23.1 11.6 %copy-start.30 = (bf16[64]{0:T(256)(128)(2,1)S(1)}, bf16[64]{0:T(256)(128)(2,1)}, u32[]{:S(2)}) copy-start(bf16[64]{0:T(256)(128)(2,1)} %param.31) | copy-start | bytes 388
  23.1 11.6 %copy-start.31 = (bf16[64]{0:T(256)(128)(2,1)S(1)}, bf16[64]{0:T(256)(128)(2,1)}, u32[]{:S(2)}) copy-start(bf16[64]{0:T(256)(128)(2,1)} %param.32) | copy-start | bytes 388
  23.1 11.6 %copy-start.32 = (bf16[256]{0:T(256)(128)(2,1)S(1)}, bf16[256]{0:T(256)(128)(2,1)}, u32[]{:S(2)}) copy-start(bf16[256]{0:T(256)(128)(2,1)} %param.34) | copy-start | bytes 1540
  23.1 11.6 %copy-start.33 = (bf16[64]{0:T(256)(128)(2,1)S(1)}, bf16[64]{0:T(256)(128)(2,1)}, u32[]{:S(2)}) copy-start(bf16[64]{0:T(256)(128)(2,1)} %param.36) | copy-start | bytes 388
  23.2 62.1 %copy-start.35 = (s32[1,8]{1,0:T(1,128)S(1)}, s32[1,8]{1,0:T(1,128)}, u32[]{:S(2)}) copy-start(s32[1,8]{1,0:T(1,128)} %param.20) | copy-start | bytes 100
  23.2 62.4 %copy-start.24 = (f32[256]{0:T(256)S(1)}, f32[256]{0:T(256)}, u32[]{:S(2)}) copy-start(f32[256]{0:T(256)} %param.22) | copy-start | bytes 3076
  23.2 62.5 %copy-start.23 = (bf16[16,1024]{1,0:T(8,128)(2,1)S(1)}, bf16[16,1024]{1,0:T(8,128)(2,1)}, u32[]{:S(2)}) copy-start(bf16[16,1024]{1,0:T(8,128)(2,1)} %param.24) | copy-start | bytes 98308
  30.7 89.1 %copy-start.21 = (bf16[256,256]{1,0:T(8,128)(2,1)S(1)}, bf16[256,256]{1,0:T(8,128)(2,1)}, u32[]{:S(2)}) copy-start(bf16[256,256]{1,0:T(8,128)(2,1)} %param.21) | copy-start | bytes 393220
  30.8 129.2 %all-gather.9.cloned.1.call-start = ((), (), s32[]{:S(2)}) async-start(), calls=%async_computation.7 | async-start | bytes 6684672 | tf_op jit(solution)/shard_map/all_gather | solution.py:158
  31.5 170.0 %all-gather.11.cloned.1.call-start = ((), (), s32[]{:S(2)}) async-start(), calls=%async_computation.8 | async-start | bytes 2228224 | tf_op jit(solution)/shard_map/all_gather | solution.py:159
  32.2 245.6 %all-gather.13.cloned.1.call-start = ((), (), s32[]{:S(2)}) async-start(), calls=%async_computation.9 | async-start | bytes 8912896 | tf_op jit(solution)/shard_map/all_gather | solution.py:160
  32.8 320.4 %all-gather.15.cloned.1.call-start = ((), (), s32[]{:S(2)}) async-start(), calls=%async_computation.10 | async-start | bytes 8912896 | tf_op jit(solution)/shard_map/all_gather | solution.py:161
  33.4 486.0 %reduce-scatter.9.cloned.1.call-start = ((), (), s32[]{:S(2)}) async-start(), calls=%async_computation.12 | async-start | bytes 557056 | tf_op jit(solution)/shard_map/reduce_scatter | solution.py:244
  118.7 46.0 %copy-start.3 = (bf16[256,1024]{1,0:T(8,128)(2,1)}, bf16[256,1024]{1,0:T(8,128)(2,1)S(1)}, u32[]{:S(2)}) copy-start(bf16[256,1024]{1,0:T(8,128)(2,1)S(1)} %all_gather.31) | copy-start | bytes 1572868
  166.0 2.9 copy-start.17
  166.2 2.7 copy-start.14
  168.3 2.0 copy-start
  171.2 106.6 %copy-start.18 = (bf16[16,64,256]{2,1,0:T(8,128)(2,1)}, bf16[16,64,256]{2,1,0:T(8,128)(2,1)S(1)}, u32[]{:S(2)}) copy-start(bf16[16,64,256]{2,1,0:T(8,128)(2,1)S(1)} %fusion.48) | copy-start | bytes 1572868
  277.8 75.4 %copy-start.7 = (bf16[256,1024]{1,0:T(8,128)(2,1)S(1)}, bf16[256,1024]{1,0:T(8,128)(2,1)}, u32[]{:S(2)}) copy-start(bf16[256,1024]{1,0:T(8,128)(2,1)} %param.37) | copy-start | bytes 1572868
  353.2 11.8 %copy-start.34 = (bf16[1024,4096]{1,0:T(8,128)(2,1)S(1)}, bf16[1024,4096]{1,0:T(8,128)(2,1)}, u32[]{:S(2)}) copy-start(bf16[1024,4096]{1,0:T(8,128)(2,1)} %all-gather.13.cloned.1.call-done) | copy-start | bytes 25165828
  365.0 2.7 copy-start.11
  365.0 3.2 copy-start.8
  367.7 1.6 copy-start.16
  368.5 0.8 copy-start.15
  372.9 4.1 copy-start.1
  372.9 4.1 copy-start.2
  396.2 5.9 copy-start.9
  401.6 1.6 copy-start.19
  402.4 5.7 copy-start.13
  402.4 5.7 copy-start.22
  404.5 121.8 %reduce-scatter.13.cloned.1.call-start = ((), (), s32[]{:S(2)}) async-start(), calls=%async_computation.14 | async-start | bytes 2228224 | tf_op jit(solution)/shard_map/reduce_scatter | solution.py:244
  408.0 204.6 %reduce-scatter.11.cloned.1.call-start = ((), (), s32[]{:S(2)}) async-start(), calls=%async_computation.13 | async-start | bytes 6684672 | tf_op jit(solution)/shard_map/reduce_scatter | solution.py:244
  413.9 1.6 copy-start.12
  413.9 307.4 %reduce-scatter.15.cloned.1.call-start = ((), (), s32[]{:S(2)}) async-start(), calls=%async_computation.15 | async-start | bytes 8912896 | tf_op jit(solution)/shard_map/reduce_scatter | solution.py:244
  421.2 1.0 copy-start.10
  421.3 408.4 %reduce-scatter.17.cloned.1.call-start = ((), (), s32[]{:S(2)}) async-start(), calls=%async_computation.16 | async-start | bytes 8912896 | tf_op jit(solution)/shard_map/reduce_scatter | solution.py:244
  429.6 1.0 copy-start.4
  429.6 1.2 copy-start.6
  429.6 2.4 copy-start.25
  429.6 464.8 %all-gather.17.cloned.1.call-start = ((), (), s32[]{:S(2)}) async-start(), calls=%async_computation.11 | async-start | bytes 4325376 | tf_op jit(solution)/shard_map/all_gather | solution.py:234
  431.9 515.1 %all-reduce.4.cloned.1.call-start = ((), (), s32[]{:S(2)}) async-start(), calls=%async_computation.17 | async-start | bytes 3145728 | tf_op jit(solution)/shard_map/psum | solution.py:247
  512.1 382.3 %copy-start.20 = (bf16[2000,256]{1,0:T(8,128)(2,1)S(1)}, bf16[2000,256]{1,0:T(8,128)(2,1)}, u32[]{:S(2)}) copy-start(bf16[2000,256]{1,0:T(8,128)(2,1)} %param.23) | copy-start | bytes 3072004
  (1 other events, 0.8 us)
Sparse Core Ops, SparseCore 0:
  30.9 62.9 reduce-scatter.6
  96.4 63.5 all-gather.8
  162.4 39.0 all-gather.10
  203.7 74.0 all-gather.12
  280.0 73.1 all-gather.14
  404.6 53.1 reduce-scatter.8
  461.5 60.8 reduce-scatter.12
  526.9 85.6 reduce-scatter.10
  616.7 104.5 reduce-scatter.14
  725.2 104.4 reduce-scatter.16
  833.2 61.2 all-gather.16
  896.8 50.2 all-reduce.3

commit v2 on v1

--- a/solution.py
+++ b/solution.py
@@ -1,6 +1,8 @@
 import jax
 import jax.numpy as jnp
 from jax import lax
+from jax.experimental import pallas as pl
+from jax.experimental.pallas import tpu as pltpu
 from jax.sharding import PartitionSpec as P
 
 HEADS = 16
@@ -281,6 +283,1000 @@
     )
 
 
+BF = jnp.bfloat16
+F32 = jnp.float32
+MESH_ID = pl.DeviceIdType.MESH
+SEM_COUNT = 400
+VMEM_LIMIT = 63 * 2**20
+NT = (((1,), (1,)), ((), ()))
+TN = (((0,), (0,)), ((), ()))
+DIAG, ACROSS, TWIN = 0, 1, 2
+FLIPS = ((1, 1), (1, 0), (0, 1))
+
+
+def mm(a, b):
+    return jnp.dot(a, b, preferred_element_type=F32)
+
+
+def mm_nt(a, b):
+    return lax.dot_general(a, b, NT, preferred_element_type=F32)
+
+
+def mm_tn(a, b):
+    return lax.dot_general(a, b, TN, preferred_element_type=F32)
+
+
+def part(start, size):
+    return pl.ds(pl.multiple_of(start, size), size)
+
+
+def as_row(pair):
+    return jnp.concatenate([pair[0:1, :], pair[1:2, :]], axis=1)
+
+
+def as_col(pair):
+    eye = lax.broadcasted_iota(jnp.int32, (128, 128), 0) == lax.broadcasted_iota(
+        jnp.int32, (128, 128), 1
+    )
+    cols = [
+        jnp.sum(jnp.where(eye, pair[k : k + 1, :], 0.0), axis=1, keepdims=True) for k in (0, 1)
+    ]
+    return jnp.concatenate(cols, axis=0)
+
+
+def norm_parts(v):
+    centred = v - jnp.mean(v, axis=-1, keepdims=True)
+    rstd = lax.rsqrt(jnp.mean(centred * centred, axis=-1, keepdims=True) + norm_eps)
+    return centred * rstd, rstd
+
+
+def norm_back(u, n, rstd):
+    return rstd * (
+        u - jnp.mean(u, axis=-1, keepdims=True) - n * jnp.mean(u * n, axis=-1, keepdims=True)
+    )
+
+
+def layer_kernel(
+    small, noise, table, w_in, w_qkv, w_out, w_up, w_down, cot,
+    act, ngrad, tgrad, vout, f_in, f_qkv, f_out, f_up, f_dn,
+    sm, smx, gsm, vec, vg, vq, vgy, vgz, vgf, bup, lives, idr,
+    tp, tok, sc, win, wqkv, wout, wup, wdn, s_in, s_qkv, s_out, s_up,
+    rin, rmid, gmid, t1, t2, t3, t4, na, proj, pr, att, asend, nb, gd, hid, ga,
+    xs, xr, gatt, gos, go, g_in, g_qkv, g_out, g_dn,
+    y_in, y_qkv, y_out, y_up, y_dn, z_in, z_qkv, z_out, z_up, z_dn, wis, wir,
+    ss, rr, ls, credit,
+):
+    x = lax.axis_index("dp")
+    f = lax.axis_index("fsdp")
+    z, y, c = f // 4, lax.rem(f // 2, 2), lax.rem(f, 2)
+    q = 2 * z + y
+    g = 2 * x + c
+    rows_here = table.shape[0]
+
+    def dev(dx, dz, dy, dc):
+        xx = lax.rem(x + dx, 2)
+        zz = lax.rem(z + dz, 4)
+        yy = lax.rem(y + dy, 2)
+        cc = lax.rem(c + dc, 2)
+        return (xx, zz * 4 + yy * 2 + cc)
+
+    twin = dev(0, 0, 0, 1)
+    across = dev(1, 0, 0, 0)
+    pair_y = dev(0, 0, 1, 0)
+    rel_dev = [dev(dx, 0, 0, dc) for dx, dc in FLIPS]
+    rel_g = [2 * lax.rem(x + dx, 2) + lax.rem(c + dc, 2) for dx, dc in FLIPS]
+    other_c = 1 - c
+
+    def far(d):
+        return lax.rem(z + 4 - d, 4)
+
+    def to(d):
+        return lax.rem(z + d, 4)
+
+    sems = [0]
+    pending = []
+
+    class Link:
+        def __init__(self):
+            self.at = sems[0]
+            sems[0] += 1
+            assert sems[0] <= SEM_COUNT
+
+        def send(self, src, dst, device):
+            self.copy = pltpu.make_async_remote_copy(
+                src_ref=src, dst_ref=dst, send_sem=ss.at[self.at], recv_sem=rr.at[self.at],
+                device_id=device, device_id_type=MESH_ID,
+            )
+            self.copy.start()
+            pending.append(self)
+            return self
+
+        def sent(self):
+            pending.remove(self)
+            self.copy.wait_send()
+
+        def got(self, ref):
+            pltpu.make_async_remote_copy(
+                src_ref=ref, dst_ref=ref, send_sem=ss.at[self.at], recv_sem=rr.at[self.at],
+                device_id=twin, device_id_type=MESH_ID,
+            ).wait_recv()
+
+    def each_rows(count, size, body):
+        def step(i, carry):
+            body(part(i * size, size))
+            return carry
+
+        lax.fori_loop(0, count // size, step, 0)
+
+    def each(count, body):
+        def step(i, carry):
+            body(i)
+            return carry
+
+        lax.fori_loop(0, count, step, 0)
+
+    barrier = pltpu.get_barrier_semaphore()
+    peers = [dev(0, d, 0, dc) for d in (1, 2, 3) for dc in (0, 1)] + rel_dev + [pair_y]
+    for peer in peers:
+        pl.semaphore_signal(barrier, inc=1, device_id=peer, device_id_type=MESH_ID)
+    pl.semaphore_wait(barrier, len(peers))
+
+    class Gather:
+        def __init__(self, whole, mine, theirs, height, twins=None):
+            self.whole, self.height = whole, height
+            places = (self.sub(q, c), self.sub(q, c, twins))
+            self.z_links = {}
+            for d in (0, 1, 2, 3):
+                for dc in (0, 1):
+                    if (d, dc) == (0, 0):
+                        continue
+                    link = Link()
+                    link.send(theirs if dc else mine, places[dc], dev(0, d, 0, dc))
+                    self.z_links[d, dc] = link
+
+        def sub(self, block, core, whole=None):
+            whole = self.whole if whole is None else whole
+            if self.height is None:
+                return whole.at[block, core]
+            return whole.at[block, part(core * self.height, self.height)]
+
+        def forward(self):
+            self.y_links = []
+            for d in (0, 1, 2, 3):
+                block = 2 * far(d) + y
+                for dc in (0, 1):
+                    if (d, dc) != (0, 0):
+                        self.z_links[d, dc].got(self.sub(block, other_c if dc else c))
+                self.y_links.append(
+                    Link().send(self.whole.at[block], self.whole.at[block], pair_y)
+                )
+
+        def finish(self):
+            for d in (0, 1, 2, 3):
+                self.y_links[d].got(self.whole.at[2 * far(d) + 1 - y])
+
+    sm[q, c] = small[...]
+    small_links = [Link().send(small, gsm.at[rel], rel_dev[rel]) for rel in (DIAG, ACROSS)]
+    gather_small = Gather(sm, small, small, None)
+
+    own_rows = tp.at[c, pl.ds(0, rows_here)]
+    own_table = pltpu.make_async_copy(table, own_rows, ls.at[0])
+    own_table.start()
+    table_link = Link().send(table, own_rows, twin)
+    spare = tp.shape[1] - rows_here
+    if spare:
+        for core in (0, 1):
+            tp[core, pl.ds(rows_here, spare), :] = jnp.zeros((spare, tp.shape[2]), BF)
+
+    def pack(whole, spare_buf, height, pick):
+        mine, theirs = pick(g), pick(2 * x + other_c)
+        whole[q, part(c * height, height), :] = mine
+        spare_buf[...] = theirs
+
+    h = w_qkv.shape[0]
+    hin = w_in.shape[0]
+
+    def cols(ref, start, size=256):
+        return ref[:, part(start, size)]
+
+    win_at, wout_at = win.at[g], wout.at[g]
+    win_at[q, c] = cols(w_in, 256 * g)
+    s_in[0] = cols(w_in, 256 * (2 * x + other_c))
+    gather_in = Gather(win_at, win_at.at[q, c], s_in.at[0], None, win.at[2 * x + other_c])
+    pack(
+        wqkv, s_qkv, h,
+        lambda k: jnp.concatenate([cols(w_qkv, 1024 * n + 256 * k) for n in (0, 1, 2)], axis=1),
+    )
+    gather_qkv = Gather(wqkv, wqkv.at[q, part(c * h, h)], s_qkv, h)
+
+
+    lives[:, 0:1] = jnp.where(as_col(small[18:20, :]) < 7.5, 1.0, 0.0)
+    vg[...] = jnp.zeros_like(vg)
+
+    def grad_down_rows(at):
+        masked = cot[at, :].astype(F32) * lives[at, 0:1]
+        gd[g, at, :] = masked.astype(BF)
+        vg[6:7, :] += jnp.sum(masked, axis=0, keepdims=True)
+
+    each_rows(256, 32, grad_down_rows)
+    gd_links = [Link().send(gd.at[g], gd.at[g], rel_dev[rel]) for rel in range(3)]
+
+    gather_small.forward()
+    pack(wout_at, s_out, h, lambda k: cols(w_out, 256 * k))
+    gather_out = Gather(
+        wout_at, wout_at.at[q, part(c * h, h)], s_out, h, wout.at[2 * x + other_c]
+    )
+
+    gather_small.finish()
+    smx_link = Link().send(sm, smx, across)
+    own_table.wait()
+    table_link.got(tp.at[other_c, pl.ds(0, rows_here)])
+    lane = lax.broadcasted_iota(jnp.int32, (256, tp.shape[1]), 1)
+
+    def look_up(block):
+        ids = as_col(sm[block, c, 16:18, :]).astype(jnp.int32)
+        total = jnp.zeros((256, 256), F32)
+        for core in (0, 1):
+            first = (4 * z + 2 * y + core) * rows_here
+            hit = jnp.where(lane == ids - first, 1.0, 0.0).astype(BF)
+            total += mm(hit, tp[core])
+        return total.astype(BF)
+
+    emb_y = [Link() for _ in range(4)]
+    for d in range(4):
+        tok[d] = look_up(2 * to(d) + 1 - y)
+        emb_y[d].send(tok.at[d], tok.at[8 + d], pair_y)
+
+    def own_blocks(d):
+        tok[4 + d] = look_up(2 * lax.rem(z + d, 4) + y)
+
+    each(4, own_blocks)
+    emb_z = [None]
+    for d in (1, 2, 3):
+        emb_y[d].got(tok.at[8 + d])
+        tok[4 + d] = tok[4 + d] + tok[8 + d]
+        emb_z.append(Link().send(tok.at[4 + d], tok.at[11 + d], dev(0, d, 0, 0)))
+    emb_y[0].got(tok.at[8])
+    gather_in.forward()
+    gather_qkv.forward()
+
+    ct = lax.broadcasted_iota(jnp.int32, (h, 128), 1) < 64
+    for j in range(8):
+        first = w_up[:, part(128 * (4 * j + x), 128)].astype(F32)
+        second = w_up[:, part(128 * (4 * j + 2 + x), 128)].astype(F32)
+        low = jnp.where(ct, first, pltpu.roll(second, 64, 1)).astype(BF)
+        high = jnp.where(ct, pltpu.roll(first, 64, 1), second).astype(BF)
+        wup[q, part(c * h, h), 128 * j : 128 * j + 128] = jnp.where(c == 0, low, high)
+        s_up[:, 128 * j : 128 * j + 128] = jnp.where(c == 0, high, low)
+    gather_up = Gather(wup, wup.at[q, part(c * h, h)], s_up, h)
+    wdn[q, part(c * h, h), :] = w_down[part(g * h, h), :]
+    gather_dn = Gather(
+        wdn, w_down.at[part(g * h, h)], w_down.at[part((2 * x + other_c) * h, h)], h
+    )
+
+    for j in range(8):
+        vec[:, 128 * j : 128 * j + 128] = sm[j, 0, 0:16, :] + sm[j, 1, 0:16, :]
+
+    rows_sum = tok[4].astype(F32) + tok[8].astype(F32)
+    for d in (1, 2, 3):
+        emb_z[d].got(tok.at[11 + d])
+        rows_sum += tok[11 + d].astype(F32)
+    for d in range(4):
+        emb_y[d].sent()
+    for d in (1, 2, 3):
+        emb_z[d].sent()
+    level = as_col(small[20:22, :])
+    scale_in = lax.rsqrt(1.0 + level * level)
+    embedded = rows_sum * lax.rsqrt(jnp.mean(rows_sum * rows_sum, axis=1, keepdims=True) + norm_eps)
+    sc[g] = ((embedded + level * noise[...].astype(F32)) * scale_in).astype(BF)
+    sc_links = [Link().send(sc.at[g], sc.at[g], rel_dev[rel]) for rel in range(3)]
+
+    gather_in.finish()
+    in_links = [Link().send(win_at, win_at, rel_dev[rel]) for rel in range(3)]
+    gather_out.forward()
+    for rel in (TWIN, ACROSS, DIAG):
+        in_links[rel].got(win.at[rel_g[rel]])
+
+    def win_mat(k):
+        return win[k].reshape(256, 256)
+
+    def first_norm(row, keep):
+        for k in range(4):
+            keep[:, 256 * k : 256 * k + 256] = (
+                mm(sc[row], win_mat(k)) + vec[0:1, 256 * k : 256 * k + 256]
+            )
+
+        def chunk(at):
+            n, _ = norm_parts(keep[at, :])
+            na[row, at, :] = (n * vec[1:2, :] + vec[2:3, :]).astype(BF)
+
+        each_rows(256, 32, chunk)
+
+    def project(row):
+        def block(k):
+            at = part(k * 256, 256)
+            proj[row, :, at] = mm(na[row], wqkv[:, :, at].reshape(1024, 256)).astype(BF)
+
+        each(3, block)
+
+    first_norm(g, rin)
+    gather_qkv.finish()
+    project(g)
+    for rel in (TWIN, ACROSS, DIAG):
+        sc_links[rel].got(sc.at[rel_g[rel]])
+        first_norm(rel_g[rel], t1)
+        project(rel_g[rel])
+
+    gather_out.finish()
+    out_links = [Link().send(wout_at, wout_at, rel_dev[rel]) for rel in range(3)]
+
+    head_of = lax.broadcasted_iota(jnp.int32, (1, 256), 1) // 64
+    small_links[DIAG].got(gsm.at[DIAG])
+    small_links[ACROSS].got(gsm.at[ACROSS])
+
+    def attend(row, pair):
+        same = as_col(pair) == as_row(pair)
+        keys = proj[row, :, 256:512]
+        values = proj[row, :, 512:768]
+        queries = proj[row, :, 0:256]
+        t2[...] = jnp.zeros_like(t2)
+
+        def head(k):
+            mine = head_of == k
+            q_head = jnp.where(mine, queries, jnp.zeros_like(queries))
+            scores = jnp.where(same, mm_nt(q_head, keys) * 0.125, -1e9)
+            weights = jnp.exp(scores - jnp.max(scores, axis=-1, keepdims=True))
+            low_probs = (weights / jnp.sum(weights, axis=-1, keepdims=True)).astype(BF)
+            pr[row * 4 + k] = low_probs
+            t2[...] += mm(low_probs, jnp.where(mine, values, jnp.zeros_like(values)))
+
+        each(4, head)
+        return t2[...].astype(BF)
+
+    att_links = []
+    my_cols = part(256 * g, 256)
+    for rel in range(3):
+        pair = sm[q, other_c, 18:20, :] if rel == TWIN else gsm[rel, 18:20, :]
+        asend[rel] = attend(rel_g[rel], pair)
+        att_links.append(Link().send(asend.at[rel], att.at[:, my_cols], rel_dev[rel]))
+    att[:, my_cols] = attend(g, small[18:20, :])
+    gather_up.forward()
+
+    for rel in (TWIN, ACROSS, DIAG):
+        out_links[rel].got(wout.at[rel_g[rel]])
+    for rel in (TWIN, ACROSS, DIAG):
+        att_links[rel].got(att.at[:, part(256 * rel_g[rel], 256)])
+
+    def out_block(k):
+        at = part(k * 256, 256)
+        rmid[:, at] = rin[:, at] + mm(att[...], wout[k].reshape(1024, 256)) + vec[3:4, at]
+
+    each(4, out_block)
+
+    def second_norm(at):
+        n, _ = norm_parts(rmid[at, :])
+        nb[g, at, :] = (n * vec[4:5, :] + vec[5:6, :]).astype(BF)
+
+    each_rows(256, 32, second_norm)
+    nb_across = Link().send(nb.at[g], nb.at[g], across)
+    nb_twin = Link().send(nb.at[g], nb.at[g], twin)
+    nb_pass = Link()
+    gather_dn.forward()
+    for rel in range(3):
+        gd_links[rel].got(gd.at[rel_g[rel]])
+
+    bup[...] = jnp.zeros_like(bup)
+    for k in range(4):
+        bup[0:1, :] += jnp.where(g == k, vec[7 + k : 8 + k, :], 0.0)
+
+    def ff_row(row):
+        def block(k):
+            at = part(k * 256, 256)
+            t2[...] = mm(nb[row], wup[:, :, at].reshape(1024, 256)) + bup[0:1, at]
+            t3[...] = mm_nt(gd[row], wdn[pl.ds(2 * k, 2)].reshape(256, 1024))
+
+            def chunk(rows_at):
+                pre = t2[rows_at, :]
+                cdf = 0.5 + 0.5 * lax.erf(pre * 0.7071067811865476)
+                pdf = jnp.exp(-0.5 * pre * pre) * 0.3989422804014327
+                t2[rows_at, :] = pre * cdf
+                ga_low = (t3[rows_at, :] * (cdf + pre * pdf)).astype(BF)
+                ga[row, rows_at, at] = ga_low
+                bup[1:2, at] += jnp.sum(ga_low.astype(F32), axis=0, keepdims=True)
+
+            each_rows(256, 32, chunk)
+            hid[pl.ds(2 * row, 2), :, at] = t2[...].astype(BF).reshape(2, 128, 256)
+
+        each(4, block)
+
+    gather_up.finish()
+    gather_dn.finish()
+    ff_row(g)
+    nb_twin.got(nb.at[rel_g[TWIN]])
+    ff_row(rel_g[TWIN])
+    nb_across.got(nb.at[rel_g[ACROSS]])
+    nb_pass.send(nb.at[rel_g[ACROSS]], nb.at[rel_g[ACROSS]], twin)
+    ff_row(rel_g[ACROSS])
+    nb_pass.got(nb.at[rel_g[DIAG]])
+    ff_row(rel_g[DIAG])
+
+    class GroupSum:
+        def __init__(self, slot, partial):
+            self.slot, self.partial = slot, partial
+
+        def first(self):
+            self.partial(rel_g[DIAG], xs.at[self.slot, 0])
+            self.a = Link().send(xs.at[self.slot, 0], xr.at[self.slot, 0], twin)
+
+        def second(self):
+            self.partial(rel_g[ACROSS], t1)
+            self.a.got(xr.at[self.slot, 0])
+
+            def chunk(at):
+                xs[self.slot, 1, at, :] = (t1[at, :] + xr[self.slot, 0, at, :].astype(F32)).astype(BF)
+
+            each_rows(256, 32, chunk)
+            self.b = Link().send(xs.at[self.slot, 1], xr.at[self.slot, 1], across)
+
+        def third(self):
+            self.partial(rel_g[TWIN], xs.at[self.slot, 2])
+            self.c = Link().send(xs.at[self.slot, 2], xr.at[self.slot, 2], twin)
+
+        def own(self, into):
+            self.partial(g, into)
+            self.into = into
+
+        def total(self):
+            self.c.got(xr.at[self.slot, 2])
+            self.b.got(xr.at[self.slot, 1])
+
+        def rows(self, at):
+            return (
+                self.into[at, :].astype(F32)
+                + xr[self.slot, 1, at, :].astype(F32)
+                + xr[self.slot, 2, at, :].astype(F32)
+            )
+
+        def release(self):
+            for link in (self.a, self.b, self.c):
+                link.sent()
+
+    def nb_partial(row, into):
+        def block(k):
+            into[:, part(k * 256, 256)] = mm_nt(
+                ga[row], wup[pl.ds(2 * k, 2)].reshape(256, 1024)
+            ).astype(into.dtype)
+
+        each(4, block)
+
+    def out_partial(row, into):
+        def block(k):
+            at = part(k * 256, 256)
+            into[:, at] = mm(
+                hid[pl.ds(2 * row, 2)].reshape(256, 1024), wdn[:, :, at].reshape(1024, 256)
+            ).astype(into.dtype)
+
+        each(4, block)
+
+    class Scatter:
+        def __init__(self, grad, y_buf, z_buf, final, height):
+            self.grad, self.y_buf, self.z_buf, self.final, self.height = (
+                grad, y_buf, z_buf, final, height,
+            )
+
+        def chunks(self, body):
+            if self.height is None:
+                each(2, body)
+            else:
+                each_rows(2 * self.height, 32, body)
+
+        def half(self, core):
+            if self.height is None:
+                return self.grad.at[q, core]
+            return self.grad.at[q, part(core * self.height, self.height)]
+
+        def start(self):
+            self.y_links = [
+                Link().send(self.grad.at[2 * to(d) + 1 - y], self.y_buf.at[d], pair_y)
+                for d in range(4)
+            ]
+
+        def middle(self):
+            self.z_links = [None]
+            for d in (1, 2, 3, 0):
+                block = 2 * to(d) + y
+                self.y_links[d].got(self.y_buf.at[d])
+
+                def chunk(at):
+                    self.grad[block, at] = (
+                        self.grad[block, at].astype(F32) + self.y_buf[d, at].astype(F32)
+                    ).astype(BF)
+
+                self.chunks(chunk)
+                if d:
+                    self.z_links.append(
+                        Link().send(self.grad.at[block], self.z_buf.at[d - 1], dev(0, d, 0, 0))
+                    )
+
+        def last(self):
+            for d in (1, 2, 3):
+                self.z_links[d].got(self.z_buf.at[d - 1])
+
+            def chunk(at):
+                total = self.grad[q, at].astype(F32)
+                for d in (0, 1, 2):
+                    total += self.z_buf[d, at].astype(F32)
+                self.grad[q, at] = total.astype(BF)
+
+            self.chunks(chunk)
+            self.f_links = []
+            for rel in range(3):
+                core = lax.rem(c + FLIPS[rel][1], 2)
+                self.f_links.append(
+                    Link().send(
+                        self.half(core),
+                        self.final.at[g],
+                        rel_dev[rel],
+                    )
+                )
+            self.final[g] = self.half(c)[...]
+
+        def finish(self):
+            for rel in range(3):
+                self.f_links[rel].got(self.final.at[rel_g[rel]])
+
+    sum_nb = GroupSum(0, nb_partial)
+    sum_nb.first()
+    sum_nb.second()
+    sum_nb.third()
+
+    scatter_dn = Scatter(g_dn, y_dn, z_dn, f_dn, h)
+    scatter_up = Scatter(hid, y_up, z_up, f_up, h)
+    sum_out = GroupSum(1, out_partial)
+
+    def dn_block(k):
+        at = part(k * 256, 256)
+        lhs = hid[:, :, at].reshape(1024, 256)
+        g_dn[pl.ds(2 * k, 2)] = mm_tn(lhs, gd[...].reshape(1024, 1024)).astype(BF).reshape(
+            2, 128, 1024
+        )
+
+    each(4, dn_block)
+    scatter_dn.start()
+    sum_out.first()
+    sum_out.second()
+    sum_out.third()
+
+    sum_out.own(act)
+
+    def up_block(k):
+        at = part(k * 256, 256)
+        lhs = nb[:, :, at].reshape(1024, 256)
+        hid[pl.ds(2 * k, 2)] = mm_tn(lhs, ga[...].reshape(1024, 1024)).astype(BF).reshape(
+            2, 128, 1024
+        )
+
+    each(4, up_block)
+    scatter_up.start()
+
+    sum_nb.own(t1)
+    sum_nb.total()
+
+    def second_back(at):
+        grad_nb = sum_nb.rows(at)
+        n, rstd = norm_parts(rmid[at, :])
+        vg[4:5, :] += jnp.sum(grad_nb * n, axis=0, keepdims=True)
+        vg[5:6, :] += jnp.sum(grad_nb, axis=0, keepdims=True)
+        mid = gd[g, at, :].astype(F32) + norm_back(grad_nb * vec[4:5, :], n, rstd)
+        gmid[at, :] = mid
+        low_mid = mid.astype(BF)
+        gatt[at, :] = low_mid
+        vg[3:4, :] += jnp.sum(low_mid.astype(F32), axis=0, keepdims=True)
+
+    each_rows(256, 32, second_back)
+
+    def grad_o_part(to_g):
+        total = jnp.zeros((256, 256), F32)
+        for k in range(4):
+            total += mm_nt(
+                gatt[:, 256 * k : 256 * k + 256], wout[k, pl.ds(2 * to_g, 2)].reshape(256, 256)
+            )
+        return total.astype(BF)
+
+    go_links = []
+    for rel in range(3):
+        gos[rel] = grad_o_part(rel_g[rel])
+        go_links.append(Link().send(gos.at[rel], go.at[g], rel_dev[rel]))
+    go[g] = grad_o_part(g)
+
+    sum_out.total()
+
+    def out_rows(at):
+        whole = rmid[at, :] + sum_out.rows(at) + vec[6:7, :]
+        act[at, :] = (whole * lives[at, 0:1]).astype(BF)
+
+    each_rows(256, 32, out_rows)
+    sum_out.release()
+    sum_nb.release()
+    for rel in range(3):
+        pl.semaphore_signal(credit, inc=1, device_id=rel_dev[rel], device_id_type=MESH_ID)
+
+    def wog(rel_slot, k):
+        for j in range(4):
+            block = mm_tn(att[:, 256 * j : 256 * j + 256], gatt[:, part(256 * k, 256)]).astype(BF)
+            if rel_slot is None:
+                g_out[2 * j : 2 * j + 2] = block.reshape(2, 128, 256)
+            else:
+                xs[1, rel_slot, :, 256 * j : 256 * j + 256] = block
+
+    for rel in range(3):
+        wog(rel, rel_g[rel])
+    wog(None, g)
+    for rel in (TWIN, ACROSS, DIAG):
+        go_links[rel].got(go.at[rel_g[rel]])
+    pl.semaphore_wait(credit, 3)
+    wog_links = [Link().send(xs.at[1, rel], xr.at[1, rel], rel_dev[rel]) for rel in range(3)]
+
+    def attend_back(row):
+        keys = proj[row, :, 256:512]
+        values = proj[row, :, 512:768]
+        queries = proj[row, :, 0:256]
+        grad_rows = go[row]
+        zero = jnp.zeros_like(keys)
+        for buf in (t2, t3, t4):
+            buf[...] = jnp.zeros_like(buf)
+
+        def head(k):
+            mine = head_of == k
+            probs = pr[row * 4 + k]
+            g_head = jnp.where(mine, grad_rows, zero)
+            t4[...] += mm_tn(probs, g_head)
+            grad_p = mm_nt(g_head, values)
+            wide = probs.astype(F32)
+            grad_s = wide * (grad_p - jnp.sum(grad_p * wide, axis=-1, keepdims=True))
+            low_s = (grad_s * 0.125).astype(BF)
+            t2[...] += mm(low_s, jnp.where(mine, keys, zero))
+            t3[...] += mm_tn(low_s, jnp.where(mine, queries, zero))
+
+        each(4, head)
+        proj[row, :, 0:256] = t2[...].astype(BF)
+        proj[row, :, 256:512] = t3[...].astype(BF)
+        proj[row, :, 512:768] = t4[...].astype(BF)
+
+    def na_partial(row, into):
+        def block(k):
+            into[:, part(k * 256, 256)] = mm_nt(
+                proj[row], wqkv[pl.ds(2 * k, 2)].reshape(256, 768)
+            ).astype(into.dtype)
+
+        each(4, block)
+
+    sum_na = GroupSum(0, na_partial)
+    attend_back(rel_g[DIAG])
+    sum_na.first()
+    attend_back(rel_g[ACROSS])
+    sum_na.second()
+    scatter_dn.middle()
+    attend_back(rel_g[TWIN])
+    sum_na.third()
+    attend_back(g)
+    sum_na.own(t1)
+
+    scatter_qkv = Scatter(g_qkv, y_qkv, z_qkv, f_qkv, h)
+    scatter_out = Scatter(g_out, y_out, z_out, f_out, h)
+    scatter_in = Scatter(g_in, y_in, z_in, f_in, None)
+
+    def qkv_block(k):
+        at = part(k * 256, 256)
+        lhs = na[:, :, at].reshape(1024, 256)
+        g_qkv[pl.ds(2 * k, 2)] = mm_tn(lhs, proj[...].reshape(1024, 768)).astype(BF).reshape(
+            2, 128, 768
+        )
+
+    each(4, qkv_block)
+    scatter_qkv.start()
+
+    for rel in range(3):
+        wog_links[rel].got(xr.at[1, rel])
+    for j in range(4):
+        block = g_out[2 * j : 2 * j + 2].reshape(256, 256).astype(F32)
+        for rel in range(3):
+            block += xr[1, rel, :, 256 * j : 256 * j + 256].astype(F32)
+        g_out[2 * j : 2 * j + 2] = block.astype(BF).reshape(2, 128, 256)
+    scatter_out.start()
+    scatter_up.middle()
+
+    sum_na.total()
+
+    def first_back(at):
+        grad_na = sum_na.rows(at)
+        n, rstd = norm_parts(rin[at, :])
+        vg[1:2, :] += jnp.sum(grad_na * n, axis=0, keepdims=True)
+        vg[2:3, :] += jnp.sum(grad_na, axis=0, keepdims=True)
+        low_in = (gmid[at, :] + norm_back(grad_na * vec[1:2, :], n, rstd)).astype(BF)
+        gatt[at, :] = low_in
+        vg[0:1, :] += jnp.sum(low_in.astype(F32), axis=0, keepdims=True)
+
+    each_rows(256, 32, first_back)
+    for k in range(4):
+        vg[7 + k : 8 + k, :] = jnp.where(g == k, bup[1:2, :], 0.0)
+    for j in range(8):
+        vq[j % 2, j // 2] = vg[:, 128 * j : 128 * j + 128]
+    vy_link = Link().send(vq.at[1 - y], vgy, pair_y)
+
+    grad_scaled = jnp.zeros((256, 256), F32)
+    for k in range(4):
+        grad_scaled += mm_nt(gatt[:, 256 * k : 256 * k + 256], win_mat(k))
+    level = as_col(small[20:22, :])
+    scale_in = lax.rsqrt(1.0 + level * level)
+    ngrad[...] = grad_scaled * (level * scale_in)
+
+    def set_at(other_x, other_y, other_core):
+        return ((lax.rem(x + other_x, 2) * 2 + lax.rem(y + other_y, 2)) * 2 + lax.rem(c + other_core, 2)) * 4
+
+    scatter_dn.last()
+    home = tok.at[set_at(0, 0, 0) + z]
+    tok[set_at(0, 0, 0) + z] = (grad_scaled * scale_in).astype(BF)
+    tok_z = [None] + [Link().send(home, home, dev(0, d, 0, 0)) for d in (1, 2, 3)]
+    tok_x = {}
+    tok_y = {}
+    tok_t = {}
+
+    def spread(spot, key, across_too):
+        ref = tok.at[spot]
+        if across_too:
+            tok_x[key] = Link().send(ref, ref, across)
+        tok_t[across_too, key] = Link().send(ref, ref, twin)
+
+    tok_y[0] = Link().send(home, home, pair_y)
+    spread(set_at(0, 0, 0) + z, (0, 0), True)
+
+    wi_links = []
+    for rel in range(3):
+        wis[rel] = mm_tn(sc[g], gatt[:, part(256 * rel_g[rel], 256)]).astype(BF)
+        wi_links.append(Link().send(wis.at[rel], wir.at[rel], rel_dev[rel]))
+    wi_own = mm_tn(sc[g], gatt[:, part(256 * g, 256)])
+
+    for d in (1, 2, 3):
+        spot = set_at(0, 0, 0) + far(d)
+        tok_z[d].got(tok.at[spot])
+        tok_y[d] = Link().send(tok.at[spot], tok.at[spot], pair_y)
+        spread(spot, (0, d), True)
+
+    for rel in range(3):
+        wi_links[rel].got(wir.at[rel])
+        wi_own += wir[rel].astype(F32)
+    g_in[...] = wi_own.astype(BF).reshape(8, 2, 16, 256)
+    scatter_in.start()
+
+    vy_link.got(vgy)
+    vq[y] = vq[y] + vgy[...]
+    vz_links = [
+        Link().send(vq.at[y, to(d)], vgz.at[d - 1], dev(0, d, 0, 0)) for d in (1, 2, 3)
+    ]
+
+    for d in range(4):
+        spot = set_at(0, 1, 0) + far(d)
+        tok_y[d].got(tok.at[spot])
+        spread(spot, (1, d), True)
+
+    scatter_qkv.middle()
+    scatter_out.middle()
+
+    for d in (1, 2, 3):
+        vz_links[d - 1].got(vgz.at[d - 1])
+    vtot = vq[y, z] + vgz[0] + vgz[1] + vgz[2]
+    vgf[3] = vtot
+    vf_links = [Link().send(vgf.at[3], vgf.at[rel], rel_dev[rel]) for rel in range(3)]
+
+    smx_link.got(smx)
+    for other_x in (0, 1):
+        for yy in (0, 1):
+            for core in (0, 1):
+                source = sm if other_x == 0 else smx
+                for zz in range(4):
+                    idr[(other_x * 2 + yy) * 2 + core : (other_x * 2 + yy) * 2 + core + 1, 256 * zz : 256 * zz + 256] = (
+                        as_row(source[2 * zz + yy, core, 16:18, :])
+                    )
+
+    tile = 400
+    base = (f * rows_here).astype(F32)
+    tile_row = lax.broadcasted_iota(jnp.int32, (tile, 1024), 0).astype(F32)
+
+    def table_add(other_x, other_y, other_core, begin):
+        spot = set_at(other_x, other_y, other_core)
+        row = (other_x * 2 + lax.rem(y + other_y, 2)) * 2 + lax.rem(c + other_core, 2)
+        ids = idr[pl.ds(row, 1), :] - base
+
+        def block(k):
+            at = part(k * tile, tile)
+            hit = jnp.where(tile_row == ids - (k * tile).astype(F32), 1.0, 0.0).astype(BF)
+            add = mm(hit, tok[pl.ds(spot, 4)].reshape(1024, 256))
+            if begin:
+                tgrad[at, :] = add
+            else:
+                tgrad[at, :] += add
+
+        each(rows_here // tile, block)
+
+    def twin_set(from_x, other_y):
+        for d in range(4):
+            tok_t[from_x == 0, (other_y, d)].got(tok.at[set_at(from_x, other_y, 1) + far(d)])
+
+    table_add(0, 0, 0, True)
+    twin_set(0, 0)
+    table_add(0, 0, 1, False)
+    scatter_up.last()
+    table_add(0, 1, 0, False)
+    twin_set(0, 1)
+    table_add(0, 1, 1, False)
+    scatter_in.middle()
+    for other_y in (0, 1):
+        for d in range(4):
+            spot = set_at(1, other_y, 0) + far(d)
+            tok_x[other_y, d].got(tok.at[spot])
+            spread(spot, (other_y, d), False)
+        table_add(1, other_y, 0, False)
+    scatter_qkv.last()
+    scatter_out.last()
+    scatter_in.last()
+    for other_y in (0, 1):
+        twin_set(1, other_y)
+        table_add(1, other_y, 1, False)
+
+    def table_rows(at):
+        values = tp[c, at, :].astype(F32)
+        r = lax.rsqrt(jnp.mean(values * values, axis=1, keepdims=True) + norm_eps)
+        row_grad = tgrad[at, :]
+        slope = jnp.mean(row_grad * values, axis=1, keepdims=True)
+        tgrad[at, :] = r * row_grad - values * (r * r * r * slope)
+
+    each_rows(rows_here, 80, table_rows)
+
+    for rel in range(3):
+        vf_links[rel].got(vgf.at[rel])
+    vout[...] = vgf[0] + vgf[1] + vgf[2] + vgf[3]
+    for scatter in (scatter_dn, scatter_up, scatter_qkv, scatter_out, scatter_in):
+        scatter.finish()
+    for link in list(pending):
+        link.sent()
+
+
+def finish_kernel(
+    act_in, ngrad_in, tgrad_in, vout, f_in, f_qkv, f_out, f_up, f_dn,
+    act, ngrad, tgrad, w_in, b_in, gain_a, shift_a, w_qkv, w_out, b_out, gain_b, shift_b,
+    w_up, b_up, w_dn, b_dn,
+):
+    c = lax.rem(lax.axis_index("fsdp"), 2)
+    act[...] = act_in[...]
+    ngrad[...] = ngrad_in[...]
+    tgrad[...] = tgrad_in[...]
+    rows = jnp.where(c == 0, vout[...], pltpu.roll(vout[...], 64, 1))
+    for k, ref in enumerate((b_in, gain_a, shift_a, b_out, gain_b, shift_b, b_dn)):
+        ref[...] = rows[k, 0:64]
+    for k in range(4):
+        b_up[64 * k : 64 * k + 64] = rows[7 + k, 0:64]
+    h = w_out.shape[0]
+    low_half = lax.broadcasted_iota(jnp.int32, (h, 128), 1) < 64
+    for g in range(4):
+        at = slice(256 * g, 256 * g + 256)
+        w_in[:, at] = f_in[g].astype(F32)
+        w_out[:, at] = f_out[g].astype(F32)
+        for n in range(3):
+            w_qkv[:, 1024 * n + 256 * g : 1024 * n + 256 * g + 256] = f_qkv[
+                g, :, 256 * n : 256 * n + 256
+            ].astype(F32)
+        w_dn[h * g : h * g + h, :] = f_dn[g].astype(F32)
+    for shard in range(16):
+        at = slice(128 * (shard // 2), 128 * (shard // 2) + 128)
+        for half in (0, 1):
+            first, second = f_up[2 * half, :, at].astype(F32), f_up[2 * half + 1, :, at].astype(F32)
+            if shard % 2 == 0:
+                both = jnp.where(low_half, first, pltpu.roll(second, 64, 1))
+            else:
+                both = jnp.where(low_half, pltpu.roll(first, 64, 1), second)
+            w_up[:, 256 * shard + 128 * half : 256 * shard + 128 * half + 128] = both
+
+
+def small_pack(seq_lengths, token_ids, noise_level, vectors, b_up):
+    tok_count = token_ids.shape[0]
+    seq_ends = jnp.cumsum(seq_lengths[0], dtype=jnp.int32)
+    positions = jnp.arange(tok_count, dtype=jnp.int32)
+    segment = jnp.sum((positions[:, None] >= seq_ends[None, :]).astype(jnp.int32), axis=1)
+    vecs = jnp.concatenate([v.reshape(1, -1) for v in vectors] + [b_up.reshape(4, -1)], axis=0)
+    vecs = vecs.astype(F32)
+    half = (jnp.arange(128) // 64) == lax.axis_index("fsdp") % 2
+    vecs = jnp.where(half[None, :], jnp.concatenate([vecs, vecs], axis=1), 0.0)
+    blank = jnp.zeros((16 - vecs.shape[0], 128), F32)
+    tail = jnp.zeros((2, 128), F32)
+    return jnp.concatenate(
+        [
+            vecs,
+            blank,
+            token_ids.astype(F32).reshape(2, 128),
+            segment.astype(F32).reshape(2, 128),
+            noise_level.reshape(2, 128),
+            tail,
+        ],
+        axis=0,
+    )
+
+
+def fused_shards(
+    token_ids, seq_lengths, noise, noise_level, table, w_in, b_in, gain_first, shift_first, w_qkv,
+    w_out, b_out, gain_second, shift_second, w_up, b_up, w_down, b_down, cotangent,
+):
+    small = small_pack(
+        seq_lengths, token_ids, noise_level,
+        (b_in, gain_first, shift_first, b_out, gain_second, shift_second, b_down), b_up,
+    )
+    vmem = pl.BlockSpec(memory_space=pltpu.VMEM)
+    hbm = pl.BlockSpec(memory_space=pl.ANY)
+
+    def shape(*dims, dtype=BF):
+        return jax.ShapeDtypeStruct(dims, dtype)
+
+    rows_here = table.shape[0]
+    padded = -(-rows_here // 256) * 256
+    outs = [
+        shape(256, 1024), shape(256, 256, dtype=F32), shape(rows_here, 256, dtype=F32),
+        shape(16, 128, dtype=F32), shape(4, 16, 256), shape(4, 64, 768), shape(4, 64, 256),
+        shape(4, 64, 1024), shape(4, 64, 1024),
+    ]
+
+    def bf(*dims):
+        return pltpu.VMEM(dims, BF)
+
+    def fl(*dims):
+        return pltpu.VMEM(dims, F32)
+
+    scratch = [
+        fl(8, 2, 24, 128), fl(8, 2, 24, 128), fl(2, 24, 128),
+        fl(16, 1024), fl(16, 1024), fl(2, 4, 16, 128), fl(4, 16, 128), fl(3, 16, 128),
+        fl(4, 16, 128), fl(8, 1024), fl(256, 128), fl(8, 1024),
+        bf(2, padded, 256), bf(32, 256, 256), bf(4, 256, 256), bf(4, 8, 2, 16, 256),
+        bf(8, 128, 768), bf(4, 8, 128, 256), bf(8, 128, 1024), bf(8, 128, 1024),
+        bf(2, 16, 256), bf(64, 768), bf(64, 256), bf(64, 1024),
+        fl(256, 1024), fl(256, 1024), fl(256, 1024), fl(256, 1024),
+        fl(256, 256), fl(256, 256), fl(256, 256),
+        bf(4, 256, 1024), bf(4, 256, 768), bf(16, 256, 256), bf(256, 1024), bf(3, 256, 256),
+        bf(4, 256, 1024), bf(4, 256, 1024), bf(8, 128, 1024), bf(4, 256, 1024),
+        bf(2, 3, 256, 1024), bf(2, 3, 256, 1024), bf(256, 1024), bf(3, 256, 256), bf(4, 256, 256),
+        bf(8, 2, 16, 256), bf(8, 128, 768), bf(8, 128, 256), bf(8, 128, 1024),
+        bf(4, 2, 16, 256), bf(4, 128, 768), bf(4, 128, 256), bf(4, 128, 1024), bf(4, 128, 1024),
+        bf(3, 2, 16, 256), bf(3, 128, 768), bf(3, 128, 256), bf(3, 128, 1024), bf(3, 128, 1024),
+        bf(3, 256, 256), bf(3, 256, 256),
+        pltpu.SemaphoreType.DMA((SEM_COUNT,)), pltpu.SemaphoreType.DMA((SEM_COUNT,)),
+        pltpu.SemaphoreType.DMA((1,)), pltpu.SemaphoreType.REGULAR,
+    ]
+    parts = pl.pallas_call(
+        layer_kernel,
+        out_shape=outs,
+        in_specs=[vmem, vmem, hbm] + [vmem] * 6,
+        out_specs=[vmem] * len(outs),
+        scratch_shapes=scratch,
+        compiler_params=pltpu.CompilerParams(
+            collective_id=0, has_side_effects=True, vmem_limit_bytes=VMEM_LIMIT
+        ),
+        cost_estimate=pl.CostEstimate(flops=40 * 10**9, bytes_accessed=30 * 10**6, transcendentals=0),
+    )(small, noise, table, w_in, w_qkv, w_out, w_up, w_down, cotangent)
+    f32 = lambda a: jax.ShapeDtypeStruct(a.shape, F32)
+    finals = [
+        outs[0], outs[1], outs[2], f32(w_in), f32(b_in), f32(gain_first), f32(shift_first),
+        f32(w_qkv), f32(w_out), f32(b_out), f32(gain_second), f32(shift_second), f32(w_up),
+        f32(b_up), f32(w_down), f32(b_down),
+    ]
+    return tuple(
+        pl.pallas_call(
+            finish_kernel,
+            out_shape=finals,
+            in_specs=[vmem] * len(outs),
+            out_specs=[vmem] * len(finals),
+            compiler_params=pltpu.CompilerParams(vmem_limit_bytes=40 * 2**20),
+        )(*parts)
+    )
+
+
 def solution(mesh):
     in_specs = (
         P(("dp", "fsdp")),
@@ -321,4 +1317,6 @@
         P("fsdp", None),
         P("fsdp"),
     )
-    return jax.shard_map(shards, mesh=mesh, in_specs=in_specs, out_specs=out_specs, check_vma=False)
+    fused = mesh.shape["dp"] == 2 and mesh.shape["fsdp"] == 16
+    body = fused_shards if fused else shards
+    return jax.shard_map(body, mesh=mesh, in_specs=in_specs, out_specs=out_specs, check_vma=False)

time: 972 us -> 326 us (0.34)
  waiting for transfers between devices: 607 us -> 0 us
  Pallas kernels: 0 us -> 306 us
  blocking collectives: 183 us -> 0 us
  matrix products: 127 us -> 0 us
  between operations: 15.9 us -> 0.7 us
  other arithmetic: 14.7 us -> 1.69 us
    pallas_call x0 -> x2, Pallas kernels: none -> 306 us  [the longest x1 303 us: fused_shards(): pl.pallas_call(layer_kernel, out_shape=outs, in_specs=[vmem, vmem, hbm] +...]
    reduce_scatter x6 -> x0, waiting for transfers between devices: 303 us -> none  [the longest x5 303 us: reduce_matrix(): lax.psum_scatter(term.astype(jnp.bfloat16), 'fsdp', scatter_dimension=0,...]
    all_gather x5 -> x0, waiting for transfers between devices: 266 us -> none  [the longest x1 73.6 us: shards(): w_up_all = lax.all_gather(w_up, 'fsdp', axis=0, tiled=True)]
    dot_general x23 -> x0, matrix products: 127 us -> none  [the longest x1 16.1 us: shards(): jnp.dot(normed_b, w_up_all, preferred_element_type=jnp.float32)]
    all_gather x3 -> x0, blocking collectives: 83.7 us -> none  [the longest x1 34.8 us: shards(): all_ids = lax.all_gather(token_ids, ('dp', 'fsdp'), axis=0, tiled=True)]
    psum x2 -> x0, blocking collectives: 49.7 us -> none  [the longest x1 43.4 us: shards(): vec_part = lax.psum(vec_term, ('dp', 'fsdp'))]
    unnamed x1 -> x0, blocking collectives: 49.5 us -> none
    psum x1 -> x0, waiting for transfers between devices: 34.4 us -> none  [reduce_matrix(): return lax.psum(part, 'dp').astype(jnp.float32)]
  transfers between devices with their start and end apart: 12 -> 0, of which waited for: 9 -> 0; matrix products, arithmetic and copies ran while one was open for 9% -> 0% of each run, Pallas kernels for 0% -> 0%
where the time goes in v2:
time: 326 us; the launch traced here: 322 us
  Pallas kernels  306 us (94%)
  local copies, waits for them, and re-layouts  13.8 us (4%)
    pallas_call x1, Pallas kernels, fused_shards(): pl.pallas_call(layer_kernel, out_shape=outs, in_specs=[vmem, vmem, hbm] +...  303 us
    unnamed x18, local copies, waits for them, and re-layouts  8.99 us

profile of v2, /device:TPU:15, one launch (start us, length us, event | category | flops | bytes accessed | tf_op | source)
XLA Modules:
  0.0 322.2 jit_solution(7851613635116116416)
XLA Ops:
  0.7 0.8 reduce-window.8
  1.5 0.1 convert_reduce_fusion
  1.6 0.7 reshape.110
  2.3 0.7 convert_bitcast_fusion
  3.0 0.9 concatenate.12
  3.9 0.1 convert_select_fusion
  4.0 3.2 concatenate.15.small
  7.1 303.3 %shard_map.306 = (bf16[256,1024]{1,0:T(8,128)(2,1)}, f32[256,256]{1,0:T(8,128)}, f32[2000,256]{1,0:T(8,128)}, f32[16,128]{1,0:T(8,128)}, bf16[4,16,256]{2,1,0:T(...) custom-call(f32[24,128]{1,0:T(8,128)} %concatenate.15.small, ...), custom_call_target="tpu_custom_call" | custom-call | flops 40000000000 | bytes 30000000 | tf_op jit(solution)/shard_map/pallas_call | solution.py:1252
  310.4 0.0 copy-start
  310.4 1.6 copy-done
  312.0 0.0 copy-start.1
  312.0 1.0 copy-done.1
  313.0 0.0 copy-start.2
  313.0 1.0 copy-done.2
  314.1 0.0 copy-start.3
  314.1 1.0 copy-done.3
  315.1 0.0 copy-start.4
  315.1 1.0 copy-done.4
  316.1 0.0 copy-start.5
  316.1 0.9 copy-done.5
  317.1 0.0 copy-start.6
  317.1 0.9 copy-done.6
  318.0 0.0 copy-start.7
  318.0 0.8 copy-done.7
  318.7 0.0 copy-start.8
  318.7 0.7 copy-done.8
  319.4 2.8 shard_map.307
  (3 shorter events, 0.0 us)
Async XLA Ops:
  310.4 1.6 copy-start
  312.0 1.0 copy-start.1
  313.0 1.0 copy-start.2
  314.1 1.0 copy-start.3
  315.1 1.0 copy-start.4
  316.1 0.9 copy-start.5
  317.1 0.9 copy-start.6
  318.0 0.8 copy-start.7
  318.7 0.7 copy-start.8

commit v3 on v2

--- a/solution.py
+++ b/solution.py
@@ -337,7 +337,9 @@
 
 
 def layer_kernel(
-    small, noise, table, w_in, w_qkv, w_out, w_up, w_down, cot,
+    small_hbm, noise_hbm, table, w_in_hbm, w_qkv_hbm, w_out_hbm, w_up_hbm, w_down_hbm, cot_hbm,
+    act_hbm, ngrad_hbm, tgrad_hbm, vout_hbm, f_in_hbm, f_qkv_hbm, f_out_hbm, f_up_hbm, f_dn_hbm,
+    small, noise, w_in, w_qkv, w_out, w_up, w_down, cot,
     act, ngrad, tgrad, vout, f_in, f_qkv, f_out, f_up, f_dn,
     sm, smx, gsm, vec, vg, vq, vgy, vgz, vgf, bup, lives, idr,
     tp, tok, sc, win, wqkv, wout, wup, wdn, s_in, s_qkv, s_out, s_up,
@@ -363,6 +365,7 @@
     twin = dev(0, 0, 0, 1)
     across = dev(1, 0, 0, 0)
     pair_y = dev(0, 0, 1, 0)
+    relay_to = (x, jnp.where(z == 2, 3, 0) * 4 + y * 2 + c)
     rel_dev = [dev(dx, 0, 0, dc) for dx, dc in FLIPS]
     rel_g = [2 * lax.rem(x + dx, 2) + lax.rem(c + dc, 2) for dx, dc in FLIPS]
     other_c = 1 - c
@@ -375,6 +378,8 @@
 
     sems = [0]
     pending = []
+    inner = jnp.logical_or(z == 1, z == 2)
+    outer = jnp.logical_not(inner)
 
     class Link:
         def __init__(self):
@@ -382,24 +387,35 @@
             sems[0] += 1
             assert sems[0] <= SEM_COUNT
 
-        def send(self, src, dst, device):
+        def send(self, src, dst, device, arrives=None, only=None):
+            self.only = only
             self.copy = pltpu.make_async_remote_copy(
-                src_ref=src, dst_ref=dst, send_sem=ss.at[self.at], recv_sem=rr.at[self.at],
+                src_ref=src, dst_ref=dst, send_sem=ss.at[self.at],
+                recv_sem=rr.at[self.at if arrives is None else arrives],
                 device_id=device, device_id_type=MESH_ID,
             )
-            self.copy.start()
+            if only is None:
+                self.copy.start()
+            else:
+                pl.when(only)(self.copy.start)
             pending.append(self)
             return self
 
         def sent(self):
             pending.remove(self)
-            self.copy.wait_send()
+            if self.only is None:
+                self.copy.wait_send()
+            else:
+                pl.when(self.only)(self.copy.wait_send)
 
         def got(self, ref):
-            pltpu.make_async_remote_copy(
-                src_ref=ref, dst_ref=ref, send_sem=ss.at[self.at], recv_sem=rr.at[self.at],
-                device_id=twin, device_id_type=MESH_ID,
-            ).wait_recv()
+            arrived(self.at, ref)
+
+    def arrived(at, ref):
+        pltpu.make_async_remote_copy(
+            src_ref=ref, dst_ref=ref, send_sem=ss.at[0], recv_sem=rr.at[at],
+            device_id=twin, device_id_type=MESH_ID,
+        ).wait_recv()
 
     def each_rows(count, size, body):
         def step(i, carry):
@@ -414,6 +430,24 @@
             return carry
 
         lax.fori_loop(0, count, step, 0)
+
+    local = [0]
+
+    def moved(src, dst):
+        copy = pltpu.make_async_copy(src, dst, ls.at[local[0]])
+        local[0] += 1
+        copy.start()
+        return copy
+
+    load_small = moved(small_hbm, small)
+    load_in = moved(w_in_hbm, w_in)
+    load_qkv = moved(w_qkv_hbm, w_qkv)
+    load_cot = moved(cot_hbm, cot)
+    own_table = moved(table, tp.at[c, pl.ds(0, rows_here)])
+    load_noise = moved(noise_hbm, noise)
+    load_out = moved(w_out_hbm, w_out)
+    load_up = moved(w_up_hbm, w_up)
+    load_down = moved(w_down_hbm, w_down)
 
     barrier = pltpu.get_barrier_semaphore()
     peers = [dev(0, d, 0, dc) for d in (1, 2, 3) for dc in (0, 1)] + rel_dev + [pair_y]
@@ -421,18 +455,34 @@
         pl.semaphore_signal(barrier, inc=1, device_id=peer, device_id_type=MESH_ID)
     pl.semaphore_wait(barrier, len(peers))
 
+    class GroupGather:
+        def __init__(self, at):
+            self.at = at
+            self.across = Link().send(at(g), at(g), across)
+            self.twin = Link().send(at(g), at(g), twin)
+
+        def hop(self):
+            self.across.got(self.at(rel_g[ACROSS]))
+            self.second = Link().send(self.at(rel_g[ACROSS]), self.at(rel_g[ACROSS]), twin)
+
+        def got_twin(self):
+            self.twin.got(self.at(rel_g[TWIN]))
+
+        def got_diag(self):
+            self.second.got(self.at(rel_g[DIAG]))
+
     class Gather:
         def __init__(self, whole, mine, theirs, height, twins=None):
             self.whole, self.height = whole, height
             places = (self.sub(q, c), self.sub(q, c, twins))
-            self.z_links = {}
-            for d in (0, 1, 2, 3):
-                for dc in (0, 1):
-                    if (d, dc) == (0, 0):
-                        continue
-                    link = Link()
-                    link.send(theirs if dc else mine, places[dc], dev(0, d, 0, dc))
-                    self.z_links[d, dc] = link
+            self.links = {}
+            for d in (0, 2, 1, 3):
+                only = {0: None, 2: None, 1: z != 3, 3: z != 0}[d]
+                for dc in (1, 0):
+                    if (d, dc) != (0, 0):
+                        self.links[d, dc] = Link().send(
+                            theirs if dc else mine, places[dc], dev(0, d, 0, dc), only=only
+                        )
 
         def sub(self, block, core, whole=None):
             whole = self.whole if whole is None else whole
@@ -440,28 +490,56 @@
                 return whole.at[block, core]
             return whole.at[block, part(core * self.height, self.height)]
 
+        def over_y(self, block):
+            return Link().send(self.whole.at[block], self.whole.at[block], pair_y)
+
+        def own(self):
+            self.links[0, 1].got(self.sub(q, other_c))
+            self.y_own = self.over_y(q)
+
+        def second(self):
+            block = 2 * far(2) + y
+            for dc in (1, 0):
+                ref = self.sub(block, other_c if dc else c)
+                self.links[2, dc].got(ref)
+                Link().send(
+                    ref, ref, relay_to, only=inner,
+                    arrives=jnp.where(z == 2, self.links[3, dc].at, self.links[1, dc].at),
+                )
+            self.y_second = self.over_y(block)
+
+        def near(self):
+            self.y_near = self.one(3, 1)
+
+        def last(self):
+            self.y_last = self.one(1, 3)
+
+        def one(self, low, high):
+            block = 2 * jnp.where(z < 2, far(low), far(high)) + y
+            for dc in (1, 0):
+                arrived(
+                    jnp.where(z < 2, self.links[low, dc].at, self.links[high, dc].at),
+                    self.sub(block, other_c if dc else c),
+                )
+            return self.over_y(block)
+
         def forward(self):
-            self.y_links = []
-            for d in (0, 1, 2, 3):
-                block = 2 * far(d) + y
-                for dc in (0, 1):
-                    if (d, dc) != (0, 0):
-                        self.z_links[d, dc].got(self.sub(block, other_c if dc else c))
-                self.y_links.append(
-                    Link().send(self.whole.at[block], self.whole.at[block], pair_y)
-                )
+            self.second()
+            self.near()
+            self.last()
 
         def finish(self):
-            for d in (0, 1, 2, 3):
-                self.y_links[d].got(self.whole.at[2 * far(d) + 1 - y])
-
+            self.y_own.got(self.whole.at[2 * z + 1 - y])
+            self.y_second.got(self.whole.at[2 * far(2) + 1 - y])
+            self.y_near.got(self.whole.at[2 * jnp.where(z < 2, far(3), far(1)) + 1 - y])
+            self.y_last.got(self.whole.at[2 * jnp.where(z < 2, far(1), far(3)) + 1 - y])
+
+    load_small.wait()
     sm[q, c] = small[...]
     small_links = [Link().send(small, gsm.at[rel], rel_dev[rel]) for rel in (DIAG, ACROSS)]
     gather_small = Gather(sm, small, small, None)
 
     own_rows = tp.at[c, pl.ds(0, rows_here)]
-    own_table = pltpu.make_async_copy(table, own_rows, ls.at[0])
-    own_table.start()
     table_link = Link().send(table, own_rows, twin)
     spare = tp.shape[1] - rows_here
     if spare:
@@ -480,6 +558,8 @@
         return ref[:, part(start, size)]
 
     win_at, wout_at = win.at[g], wout.at[g]
+    load_in.wait()
+    load_qkv.wait()
     win_at[q, c] = cols(w_in, 256 * g)
     s_in[0] = cols(w_in, 256 * (2 * x + other_c))
     gather_in = Gather(win_at, win_at.at[q, c], s_in.at[0], None, win.at[2 * x + other_c])
@@ -498,14 +578,12 @@
         gd[g, at, :] = masked.astype(BF)
         vg[6:7, :] += jnp.sum(masked, axis=0, keepdims=True)
 
+    load_cot.wait()
     each_rows(256, 32, grad_down_rows)
-    gd_links = [Link().send(gd.at[g], gd.at[g], rel_dev[rel]) for rel in range(3)]
-
+    group_gd = GroupGather(lambda k: gd.at[k])
+
+    gather_small.own()
     gather_small.forward()
-    pack(wout_at, s_out, h, lambda k: cols(w_out, 256 * k))
-    gather_out = Gather(
-        wout_at, wout_at.at[q, part(c * h, h)], s_out, h, wout.at[2 * x + other_c]
-    )
 
     gather_small.finish()
     smx_link = Link().send(sm, smx, across)
@@ -531,15 +609,18 @@
         tok[4 + d] = look_up(2 * lax.rem(z + d, 4) + y)
 
     each(4, own_blocks)
+    gather_in.own()
+    gather_qkv.own()
     emb_z = [None]
     for d in (1, 2, 3):
         emb_y[d].got(tok.at[8 + d])
         tok[4 + d] = tok[4 + d] + tok[8 + d]
         emb_z.append(Link().send(tok.at[4 + d], tok.at[11 + d], dev(0, d, 0, 0)))
     emb_y[0].got(tok.at[8])
-    gather_in.forward()
-    gather_qkv.forward()
-
+
+    for load in (load_noise, load_out, load_up, load_down):
+        load.wait()
+    pack(wout_at, s_out, h, lambda k: cols(w_out, 256 * k))
     ct = lax.broadcasted_iota(jnp.int32, (h, 128), 1) < 64
     for j in range(8):
         first = w_up[:, part(128 * (4 * j + x), 128)].astype(F32)
@@ -548,19 +629,27 @@
         high = jnp.where(ct, pltpu.roll(first, 64, 1), second).astype(BF)
         wup[q, part(c * h, h), 128 * j : 128 * j + 128] = jnp.where(c == 0, low, high)
         s_up[:, 128 * j : 128 * j + 128] = jnp.where(c == 0, high, low)
-    gather_up = Gather(wup, wup.at[q, part(c * h, h)], s_up, h)
     wdn[q, part(c * h, h), :] = w_down[part(g * h, h), :]
-    gather_dn = Gather(
-        wdn, w_down.at[part(g * h, h)], w_down.at[part((2 * x + other_c) * h, h)], h
-    )
-
+    gather_in.forward()
+    gather_qkv.forward()
     for j in range(8):
         vec[:, 128 * j : 128 * j + 128] = sm[j, 0, 0:16, :] + sm[j, 1, 0:16, :]
 
+    gather_in.finish()
+    group_in = GroupGather(lambda k: win.at[k])
+    group_gd.hop()
     rows_sum = tok[4].astype(F32) + tok[8].astype(F32)
     for d in (1, 2, 3):
         emb_z[d].got(tok.at[11 + d])
         rows_sum += tok[11 + d].astype(F32)
+    gather_out = Gather(
+        wout_at, wout_at.at[q, part(c * h, h)], s_out, h, wout.at[2 * x + other_c]
+    )
+    gather_up = Gather(wup, wup.at[q, part(c * h, h)], s_up, h)
+    gather_dn = Gather(
+        wdn, w_down.at[part(g * h, h)], w_down.at[part((2 * x + other_c) * h, h)], h
+    )
+
     for d in range(4):
         emb_y[d].sent()
     for d in (1, 2, 3):
@@ -569,13 +658,11 @@
     scale_in = lax.rsqrt(1.0 + level * level)
     embedded = rows_sum * lax.rsqrt(jnp.mean(rows_sum * rows_sum, axis=1, keepdims=True) + norm_eps)
     sc[g] = ((embedded + level * noise[...].astype(F32)) * scale_in).astype(BF)
-    sc_links = [Link().send(sc.at[g], sc.at[g], rel_dev[rel]) for rel in range(3)]
-
-    gather_in.finish()
-    in_links = [Link().send(win_at, win_at, rel_dev[rel]) for rel in range(3)]
-    gather_out.forward()
-    for rel in (TWIN, ACROSS, DIAG):
-        in_links[rel].got(win.at[rel_g[rel]])
+    group_sc = GroupGather(lambda k: sc.at[k])
+
+    group_in.hop()
+    group_in.got_twin()
+    group_in.got_diag()
 
     def win_mat(k):
         return win[k].reshape(256, 256)
@@ -600,15 +687,22 @@
         each(3, block)
 
     first_norm(g, rin)
+    group_sc.hop()
+    gather_out.own()
+    gather_out.forward()
+    gather_up.own()
+    gather_dn.own()
+    group_sc.got_twin()
+    first_norm(rel_g[TWIN], t1)
+    first_norm(rel_g[ACROSS], t1)
+    group_sc.got_diag()
+    first_norm(rel_g[DIAG], t1)
     gather_qkv.finish()
+    for rel in range(3):
+        project(rel_g[rel])
     project(g)
-    for rel in (TWIN, ACROSS, DIAG):
-        sc_links[rel].got(sc.at[rel_g[rel]])
-        first_norm(rel_g[rel], t1)
-        project(rel_g[rel])
-
     gather_out.finish()
-    out_links = [Link().send(wout_at, wout_at, rel_dev[rel]) for rel in range(3)]
+    group_out = GroupGather(lambda k: wout.at[k])
 
     head_of = lax.broadcasted_iota(jnp.int32, (1, 256), 1) // 64
     small_links[DIAG].got(gsm.at[DIAG])
@@ -639,11 +733,15 @@
         pair = sm[q, other_c, 18:20, :] if rel == TWIN else gsm[rel, 18:20, :]
         asend[rel] = attend(rel_g[rel], pair)
         att_links.append(Link().send(asend.at[rel], att.at[:, my_cols], rel_dev[rel]))
+        if rel == DIAG:
+            gather_up.second()
+        if rel == TWIN:
+            gather_up.near()
+            gather_up.last()
     att[:, my_cols] = attend(g, small[18:20, :])
-    gather_up.forward()
-
-    for rel in (TWIN, ACROSS, DIAG):
-        out_links[rel].got(wout.at[rel_g[rel]])
+    group_out.hop()
+    group_out.got_twin()
+    group_out.got_diag()
     for rel in (TWIN, ACROSS, DIAG):
         att_links[rel].got(att.at[:, part(256 * rel_g[rel], 256)])
 
@@ -662,8 +760,8 @@
     nb_twin = Link().send(nb.at[g], nb.at[g], twin)
     nb_pass = Link()
     gather_dn.forward()
-    for rel in range(3):
-        gd_links[rel].got(gd.at[rel_g[rel]])
+    group_gd.got_twin()
+    group_gd.got_diag()
 
     bup[...] = jnp.zeros_like(bup)
     for k in range(4):
@@ -716,6 +814,8 @@
                 xs[self.slot, 1, at, :] = (t1[at, :] + xr[self.slot, 0, at, :].astype(F32)).astype(BF)
 
             each_rows(256, 32, chunk)
+
+        def second_send(self):
             self.b = Link().send(xs.at[self.slot, 1], xr.at[self.slot, 1], across)
 
         def third(self):
@@ -775,40 +875,92 @@
                 return self.grad.at[q, core]
             return self.grad.at[q, part(core * self.height, self.height)]
 
-        def start(self):
-            self.y_links = [
-                Link().send(self.grad.at[2 * to(d) + 1 - y], self.y_buf.at[d], pair_y)
-                for d in range(4)
-            ]
-
-        def middle(self):
-            self.z_links = [None]
-            for d in (1, 2, 3, 0):
-                block = 2 * to(d) + y
-                self.y_links[d].got(self.y_buf.at[d])
+        def start(self, count=4):
+            even = lax.rem(z, 2) == 0
+            self.goals = (
+                jnp.where(even, 3, 0), jnp.where(even, 1, 2), lax.rem(z + 2, 4), z,
+            )
+            self.y_links = []
+            self.z_links = [Link() for _ in range(4)]
+            self.more(count)
+
+        def more(self, count=1):
+            for _ in range(count):
+                e = len(self.y_links)
+                self.y_links.append(
+                    Link().send(self.grad.at[2 * self.goals[e] + 1 - y], self.y_buf.at[e], pair_y)
+                )
+
+        def add_y(self, e):
+            self.y_links[e].got(self.y_buf.at[e])
+            block = 2 * self.goals[e] + y
+
+            def chunk(at):
+                self.grad[block, at] = (
+                    self.grad[block, at].astype(F32) + self.y_buf[e, at].astype(F32)
+                ).astype(BF)
+
+            self.chunks(chunk)
+            return self.grad.at[block]
+
+        def end_to_end(self):
+            ref = self.add_y(0)
+            self.z_links[0].send(
+                ref, self.z_buf.at[0], (x, (z + 1 - 2 * lax.rem(z, 2)) * 4 + y * 2 + c)
+            )
+
+        def near(self):
+            ref = self.add_y(1)
+            slot = jnp.where(inner, 2, 1)
+            self.z_links[1].send(
+                ref, self.z_buf.at[slot], (x, self.goals[1] * 4 + y * 2 + c),
+                arrives=jnp.where(inner, self.z_links[2].at, self.z_links[1].at),
+            )
+
+        def second(self):
+            ref = self.add_y(2)
+            block = 2 * self.goals[2] + y
+
+            def relayed():
+                self.z_links[0].got(self.z_buf.at[0])
 
                 def chunk(at):
                     self.grad[block, at] = (
-                        self.grad[block, at].astype(F32) + self.y_buf[d, at].astype(F32)
+                        self.grad[block, at].astype(F32) + self.z_buf[0, at].astype(F32)
                     ).astype(BF)
 
                 self.chunks(chunk)
-                if d:
-                    self.z_links.append(
-                        Link().send(self.grad.at[block], self.z_buf.at[d - 1], dev(0, d, 0, 0))
-                    )
+
+            pl.when(inner)(relayed)
+            self.z_links[3].send(ref, self.z_buf.at[3], dev(0, 2, 0, 0))
+
+        def own(self):
+            self.add_y(3)
+
+        def middle(self):
+            self.end_to_end()
+            self.near()
+            self.second()
+            self.own()
 
         def last(self):
-            for d in (1, 2, 3):
-                self.z_links[d].got(self.z_buf.at[d - 1])
-
-            def chunk(at):
-                total = self.grad[q, at].astype(F32)
-                for d in (0, 1, 2):
-                    total += self.z_buf[d, at].astype(F32)
-                self.grad[q, at] = total.astype(BF)
-
-            self.chunks(chunk)
+            def summed(slots):
+                def run():
+                    for slot in slots:
+                        self.z_links[slot].got(self.z_buf.at[slot])
+
+                    def chunk(at):
+                        total = self.grad[q, at].astype(F32)
+                        for slot in slots:
+                            total += self.z_buf[slot, at].astype(F32)
+                        self.grad[q, at] = total.astype(BF)
+
+                    self.chunks(chunk)
+
+                return run
+
+            pl.when(inner)(summed((1, 2, 3)))
+            pl.when(outer)(summed((0, 3)))
             self.f_links = []
             for rel in range(3):
                 core = lax.rem(c + FLIPS[rel][1], 2)
@@ -828,6 +980,7 @@
     sum_nb = GroupSum(0, nb_partial)
     sum_nb.first()
     sum_nb.second()
+    sum_nb.second_send()
     sum_nb.third()
 
     scatter_dn = Scatter(g_dn, y_dn, z_dn, f_dn, h)
@@ -860,6 +1013,7 @@
     scatter_up.start()
 
     sum_nb.own(t1)
+    scatter_dn.end_to_end()
     sum_nb.total()
 
     def second_back(at):
@@ -870,7 +1024,7 @@
         mid = gd[g, at, :].astype(F32) + norm_back(grad_nb * vec[4:5, :], n, rstd)
         gmid[at, :] = mid
         low_mid = mid.astype(BF)
-        gatt[at, :] = low_mid
+        gatt[1, at, :] = low_mid
         vg[3:4, :] += jnp.sum(low_mid.astype(F32), axis=0, keepdims=True)
 
     each_rows(256, 32, second_back)
@@ -879,7 +1033,7 @@
         total = jnp.zeros((256, 256), F32)
         for k in range(4):
             total += mm_nt(
-                gatt[:, 256 * k : 256 * k + 256], wout[k, pl.ds(2 * to_g, 2)].reshape(256, 256)
+                gatt[1, :, 256 * k : 256 * k + 256], wout[k, pl.ds(2 * to_g, 2)].reshape(256, 256)
             )
         return total.astype(BF)
 
@@ -889,33 +1043,12 @@
         go_links.append(Link().send(gos.at[rel], go.at[g], rel_dev[rel]))
     go[g] = grad_o_part(g)
 
-    sum_out.total()
-
-    def out_rows(at):
-        whole = rmid[at, :] + sum_out.rows(at) + vec[6:7, :]
-        act[at, :] = (whole * lives[at, 0:1]).astype(BF)
-
-    each_rows(256, 32, out_rows)
-    sum_out.release()
+    sum_out.second_send()
     sum_nb.release()
-    for rel in range(3):
-        pl.semaphore_signal(credit, inc=1, device_id=rel_dev[rel], device_id_type=MESH_ID)
-
-    def wog(rel_slot, k):
-        for j in range(4):
-            block = mm_tn(att[:, 256 * j : 256 * j + 256], gatt[:, part(256 * k, 256)]).astype(BF)
-            if rel_slot is None:
-                g_out[2 * j : 2 * j + 2] = block.reshape(2, 128, 256)
-            else:
-                xs[1, rel_slot, :, 256 * j : 256 * j + 256] = block
-
-    for rel in range(3):
-        wog(rel, rel_g[rel])
-    wog(None, g)
+    scatter_dn.near()
+    scatter_dn.second()
     for rel in (TWIN, ACROSS, DIAG):
         go_links[rel].got(go.at[rel_g[rel]])
-    pl.semaphore_wait(credit, 3)
-    wog_links = [Link().send(xs.at[1, rel], xr.at[1, rel], rel_dev[rel]) for rel in range(3)]
 
     def attend_back(row):
         keys = proj[row, :, 256:512]
@@ -956,9 +1089,12 @@
     sum_na.first()
     attend_back(rel_g[ACROSS])
     sum_na.second()
-    scatter_dn.middle()
+    sum_na.second_send()
+    scatter_dn.own()
+    scatter_up.end_to_end()
     attend_back(rel_g[TWIN])
     sum_na.third()
+    scatter_up.near()
     attend_back(g)
     sum_na.own(t1)
 
@@ -974,17 +1110,21 @@
         )
 
     each(4, qkv_block)
-    scatter_qkv.start()
-
+    scatter_qkv.start(1)
+    scatter_up.second()
+    scatter_dn.last()
+
+    sum_out.total()
+
+    def out_rows(at):
+        whole = rmid[at, :] + sum_out.rows(at) + vec[6:7, :]
+        act[at, :] = (whole * lives[at, 0:1]).astype(BF)
+
+    each_rows(256, 32, out_rows)
+    stores = [moved(act, act_hbm)]
+    sum_out.release()
     for rel in range(3):
-        wog_links[rel].got(xr.at[1, rel])
-    for j in range(4):
-        block = g_out[2 * j : 2 * j + 2].reshape(256, 256).astype(F32)
-        for rel in range(3):
-            block += xr[1, rel, :, 256 * j : 256 * j + 256].astype(F32)
-        g_out[2 * j : 2 * j + 2] = block.astype(BF).reshape(2, 128, 256)
-    scatter_out.start()
-    scatter_up.middle()
+        pl.semaphore_signal(credit, inc=1, device_id=rel_dev[rel], device_id_type=MESH_ID)
 
     sum_na.total()
 
@@ -994,7 +1134,7 @@
         vg[1:2, :] += jnp.sum(grad_na * n, axis=0, keepdims=True)
         vg[2:3, :] += jnp.sum(grad_na, axis=0, keepdims=True)
         low_in = (gmid[at, :] + norm_back(grad_na * vec[1:2, :], n, rstd)).astype(BF)
-        gatt[at, :] = low_in
+        gatt[0, at, :] = low_in
         vg[0:1, :] += jnp.sum(low_in.astype(F32), axis=0, keepdims=True)
 
     each_rows(256, 32, first_back)
@@ -1006,15 +1146,15 @@
 
     grad_scaled = jnp.zeros((256, 256), F32)
     for k in range(4):
-        grad_scaled += mm_nt(gatt[:, 256 * k : 256 * k + 256], win_mat(k))
+        grad_scaled += mm_nt(gatt[0, :, 256 * k : 256 * k + 256], win_mat(k))
     level = as_col(small[20:22, :])
     scale_in = lax.rsqrt(1.0 + level * level)
     ngrad[...] = grad_scaled * (level * scale_in)
+    stores.append(moved(ngrad, ngrad_hbm))
 
     def set_at(other_x, other_y, other_core):
         return ((lax.rem(x + other_x, 2) * 2 + lax.rem(y + other_y, 2)) * 2 + lax.rem(c + other_core, 2)) * 4
 
-    scatter_dn.last()
     home = tok.at[set_at(0, 0, 0) + z]
     tok[set_at(0, 0, 0) + z] = (grad_scaled * scale_in).astype(BF)
     tok_z = [None] + [Link().send(home, home, dev(0, d, 0, 0)) for d in (1, 2, 3)]
@@ -1031,18 +1171,41 @@
     tok_y[0] = Link().send(home, home, pair_y)
     spread(set_at(0, 0, 0) + z, (0, 0), True)
 
+    def wog_partial(k, into):
+        for j in range(4):
+            into[:, 256 * j : 256 * j + 256] = mm_tn(
+                att[:, 256 * j : 256 * j + 256], gatt[1, :, part(256 * k, 256)]
+            ).astype(into.dtype)
+
+    pl.semaphore_wait(credit, 3)
+    sum_wog = GroupSum(1, wog_partial)
+    sum_wog.first()
+    sum_wog.second()
+    sum_wog.second_send()
+    sum_wog.third()
+    sum_wog.own(t1)
     wi_links = []
     for rel in range(3):
-        wis[rel] = mm_tn(sc[g], gatt[:, part(256 * rel_g[rel], 256)]).astype(BF)
+        wis[rel] = mm_tn(sc[g], gatt[0, :, part(256 * rel_g[rel], 256)]).astype(BF)
         wi_links.append(Link().send(wis.at[rel], wir.at[rel], rel_dev[rel]))
-    wi_own = mm_tn(sc[g], gatt[:, part(256 * g, 256)])
+    wi_own = mm_tn(sc[g], gatt[0, :, part(256 * g, 256)])
 
     for d in (1, 2, 3):
         spot = set_at(0, 0, 0) + far(d)
         tok_z[d].got(tok.at[spot])
         tok_y[d] = Link().send(tok.at[spot], tok.at[spot], pair_y)
         spread(spot, (0, d), True)
-
+        scatter_qkv.more()
+        if d == 1:
+            scatter_up.own()
+            scatter_qkv.end_to_end()
+
+    sum_wog.total()
+    for j in range(4):
+        at = slice(256 * j, 256 * j + 256)
+        block = t1[:, at] + xr[1, 1, :, at].astype(F32) + xr[1, 2, :, at].astype(F32)
+        g_out[2 * j : 2 * j + 2] = block.astype(BF).reshape(2, 128, 256)
+    scatter_out.start()
     for rel in range(3):
         wi_links[rel].got(wir.at[rel])
         wi_own += wir[rel].astype(F32)
@@ -1060,7 +1223,9 @@
         tok_y[d].got(tok.at[spot])
         spread(spot, (1, d), True)
 
-    scatter_qkv.middle()
+    scatter_qkv.near()
+    scatter_qkv.second()
+    scatter_qkv.own()
     scatter_out.middle()
 
     for d in (1, 2, 3):
@@ -1132,14 +1297,19 @@
         tgrad[at, :] = r * row_grad - values * (r * r * r * slope)
 
     each_rows(rows_here, 80, table_rows)
+    stores.append(moved(tgrad, tgrad_hbm))
 
     for rel in range(3):
         vf_links[rel].got(vgf.at[rel])
     vout[...] = vgf[0] + vgf[1] + vgf[2] + vgf[3]
     for scatter in (scatter_dn, scatter_up, scatter_qkv, scatter_out, scatter_in):
         scatter.finish()
+    for k, (src, dst) in enumerate(((f_in, f_in_hbm), (f_qkv, f_qkv_hbm), (f_out, f_out_hbm), (f_up, f_up_hbm), (f_dn, f_dn_hbm), (vout, vout_hbm))):
+        stores.append(moved(src, dst))
     for link in list(pending):
         link.sent()
+    for store in stores:
+        store.wait()
 
 
 def finish_kernel(
@@ -1224,6 +1394,9 @@
         shape(4, 64, 1024), shape(4, 64, 1024),
     ]
 
+    held = [pltpu.VMEM(v.shape, v.dtype) for v in (small, noise, w_in, w_qkv, w_out, w_up, w_down, cotangent)]
+    held += [pltpu.VMEM(v.shape, v.dtype) for v in outs]
+
     def bf(*dims):
         return pltpu.VMEM(dims, BF)
 
@@ -1241,20 +1414,20 @@
         fl(256, 256), fl(256, 256), fl(256, 256),
         bf(4, 256, 1024), bf(4, 256, 768), bf(16, 256, 256), bf(256, 1024), bf(3, 256, 256),
         bf(4, 256, 1024), bf(4, 256, 1024), bf(8, 128, 1024), bf(4, 256, 1024),
-        bf(2, 3, 256, 1024), bf(2, 3, 256, 1024), bf(256, 1024), bf(3, 256, 256), bf(4, 256, 256),
+        bf(2, 3, 256, 1024), bf(2, 3, 256, 1024), bf(2, 256, 1024), bf(3, 256, 256), bf(4, 256, 256),
         bf(8, 2, 16, 256), bf(8, 128, 768), bf(8, 128, 256), bf(8, 128, 1024),
         bf(4, 2, 16, 256), bf(4, 128, 768), bf(4, 128, 256), bf(4, 128, 1024), bf(4, 128, 1024),
-        bf(3, 2, 16, 256), bf(3, 128, 768), bf(3, 128, 256), bf(3, 128, 1024), bf(3, 128, 1024),
+        bf(4, 2, 16, 256), bf(4, 128, 768), bf(4, 128, 256), bf(4, 128, 1024), bf(4, 128, 1024),
         bf(3, 256, 256), bf(3, 256, 256),
         pltpu.SemaphoreType.DMA((SEM_COUNT,)), pltpu.SemaphoreType.DMA((SEM_COUNT,)),
-        pltpu.SemaphoreType.DMA((1,)), pltpu.SemaphoreType.REGULAR,
+        pltpu.SemaphoreType.DMA((20,)), pltpu.SemaphoreType.REGULAR,
     ]
     parts = pl.pallas_call(
         layer_kernel,
         out_shape=outs,
-        in_specs=[vmem, vmem, hbm] + [vmem] * 6,
-        out_specs=[vmem] * len(outs),
-        scratch_shapes=scratch,
+        in_specs=[hbm] * 9,
+        out_specs=[hbm] * len(outs),
+        scratch_shapes=held + scratch,
         compiler_params=pltpu.CompilerParams(
             collective_id=0, has_side_effects=True, vmem_limit_bytes=VMEM_LIMIT
         ),
@@ -1272,7 +1445,7 @@
             out_shape=finals,
             in_specs=[vmem] * len(outs),
             out_specs=[vmem] * len(finals),
-            compiler_params=pltpu.CompilerParams(vmem_limit_bytes=40 * 2**20),
+            compiler_params=pltpu.CompilerParams(vmem_limit_bytes=VMEM_LIMIT),
         )(*parts)
     )
 

time: 326 us -> 252 us (0.77)
  Pallas kernels: 306 us -> 240 us
  local copies, waits for them, and re-layouts: 13.8 us -> 4.76 us
    pallas_call x1, Pallas kernels: 303 us -> 235 us  [fused_shards(): pl.pallas_call(layer_kernel, out_shape=outs, in_specs=[hbm] * 9, out_spec...]
    unnamed x18 -> x0, local copies, waits for them, and re-layouts: 8.99 us -> none
where the time goes in v3:
time: 252 us; the launch traced here: 248 us
  Pallas kernels  240 us (95%)
  local copies, waits for them, and re-layouts  4.76 us (2%)
    pallas_call x1, Pallas kernels, fused_shards(): pl.pallas_call(layer_kernel, out_shape=outs, in_specs=[hbm] * 9, out_spec...  235 us
    pallas_call x1, Pallas kernels, fused_shards(): pl.pallas_call(finish_kernel, out_shape=finals, in_specs=[vmem] * len(out...  5.07 us

profile of v3, /device:TPU:15, one launch (start us, length us, event | category | flops | bytes accessed | tf_op | source)
XLA Modules:
  0.0 247.6 jit_solution(8202477377241281289)
XLA Ops:
  0.7 0.8 reduce-window.8
  1.5 0.1 convert_reduce_fusion
  1.6 0.7 reshape.110
  2.3 0.7 convert_bitcast_fusion
  3.0 0.9 concatenate.12
  3.9 0.1 convert_select_fusion
  4.0 3.2 %concatenate.15.small_hbm = f32[24,128]{1,0:T(8,128)} concatenate(f32[11,128]{1,0:T(8,128)S(1)} %convert_select_fusion, f32[5,128]{1,0:T(8,128)S(1)} %broadcast_in_dim.23, f32[2,128]{1,0:T(2,128)S(1)} %get-tuple-element.35, f32[2,128]{1,0:T(2,128)S(1)} %get-tuple-element.34, f32[2,128]{1,0:T(2,128)} %bitcast.14, f32[2,128]{1,0:T(2,128)S(1)} %broadcast_in_dim.24), dimensions={0} | concatenate | bytes 24576 | tf_op jit(solution)/shard_map/concatenate | solution.py:1362
  7.1 235.3 %shard_map.306 = (bf16[256,1024]{1,0:T(8,128)(2,1)}, f32[256,256]{1,0:T(8,128)}, f32[2000,256]{1,0:T(8,128)}, f32[16,128]{1,0:T(8,128)}, bf16[4,16,256]{2,1,0:T(...) custom-call(f32[24,128]{1,0:T(8,128)} %concatenate.15.small_hbm, ...), custom_call_target="tpu_custom_call" | custom-call | flops 40000000000 | bytes 30000000 | tf_op jit(solution)/shard_map/pallas_call | solution.py:1425
  242.4 5.1 %shard_map.307 = (bf16[256,1024]{1,0:T(8,128)(2,1)}, f32[256,256]{1,0:T(8,128)}, f32[2000,256]{1,0:T(8,128)}, f32[16,1024]{1,0:T(8,128)}, f32[64]{0:T(128)}, /*i...) custom-call(bf16[256,1024]{1,0:T(8,128)(2,1)} %get-tuple-element.25., ...), custom_call_target="tpu_custom_call" | custom-call | tf_op jit(solution)/shard_map/pallas_call | solution.py:1443
  (3 shorter events, 0.0 us)
